TPU v7x, 128 devices: a whole 4x4x4 slice. The times are simulated.
128 devices in a mesh: dp: 16 (over x, y), fsdp: 8 (over z, core).
Axes of the slice: x: 4, y: 4, z: 4, core: 2. Of those that a mesh axis runs over, the one named last changes fastest.
Arguments:
- source: bfloat16 [2, 128, 256, 512], P(None, ('dp', 'fsdp')), may hold values from -24 to 24
- target: bfloat16 [2, 128, 256, 512], P(None, ('dp', 'fsdp')), may hold values from -24 to 24
- src_len: int32 [2, 128], P(None, ('dp', 'fsdp')), may hold values from 21 to 256, as said below
- tgt_len: int32 [2, 128], P(None, ('dp', 'fsdp')), may hold values from 21 to 256, as said below
- out_grad: bfloat16 [2, 128, 256, 512], P(None, ('dp', 'fsdp')), may hold values from -6 to 6
- attn_proj: bfloat16 [3, 3, 512, 512], P(None, None, ('dp', 'fsdp')), may hold values from -0.25 to 0.25
- attn_out: bfloat16 [3, 512, 512], P(None, ('dp', 'fsdp')), may hold values from -1 to 1
- attn_bias: bfloat16 [3, 3, 512], P(None, None, ('dp', 'fsdp')), may hold values from -2 to 2
- norm_gain: bfloat16 [5, 512], P(None, ('dp', 'fsdp')), may hold values from 0.25 to 1.75
- norm_shift: bfloat16 [5, 512], P(None, ('dp', 'fsdp')), may hold values from -1.5 to 1.5
- ffn_in: bfloat16 [2, 512, 2048], P(None, ('dp', 'fsdp')), may hold values from -0.25 to 0.25
- ffn_out: bfloat16 [2, 2048, 512], P(None, ('dp', 'fsdp')), may hold values from -0.25 to 0.25
- ffn_bias_in: bfloat16 [2, 2048], P(None, ('dp', 'fsdp')), may hold values from -2 to 2
- ffn_bias_out: bfloat16 [2, 512], P(None, ('dp', 'fsdp')), may hold values from -2 to 2
Outputs:
- dec_out: bfloat16 [2, 128, 256, 512], P(None, ('dp', 'fsdp'))
- source_grad: float32 [2, 128, 256, 512], P(None, ('dp', 'fsdp'))
- target_grad: float32 [2, 128, 256, 512], P(None, ('dp', 'fsdp'))
- g_attn_proj: float32 [3, 3, 512, 512], P(None, None, ('dp', 'fsdp'))
- g_attn_out: float32 [3, 512, 512], P(None, ('dp', 'fsdp'))
- g_attn_bias: float32 [3, 3, 512], P(None, None, ('dp', 'fsdp'))
- g_norm_gain: float32 [5, 512], P(None, ('dp', 'fsdp'))
- g_norm_shift: float32 [5, 512], P(None, ('dp', 'fsdp'))
- g_ffn_in: float32 [2, 512, 2048], P(None, ('dp', 'fsdp'))
- g_ffn_out: float32 [2, 2048, 512], P(None, ('dp', 'fsdp'))
- g_ffn_bias_in: float32 [2, 2048], P(None, ('dp', 'fsdp'))
- g_ffn_bias_out: float32 [2, 512], P(None, ('dp', 'fsdp'))
Inputs may be any that keep to these rules, and one draw needn't show every extreme that they name: `src_len`: most sentences are short, a few have up to 256 tokens; 256 is reached by some source sentence in every draw. `tgt_len`: most sentences are short, a few have up to 256 tokens; 256 is reached by some target sentence in every draw.
All inputs are finite; a program needn't handle non-finite values.
Results may differ from a plain program's by a relative error of at most 0.025.
Values may be sent and summed in bfloat16 or wider, within the bound.
No kernel may reach another device: no remote copies, remote signals or barrier semaphores. Data moves between devices by JAX's collectives and lax.ppermute only.
A program may use at most 192 MiB of HBM per device.

v0:
```python
import functools

import jax
import jax.numpy as jnp
from jax import lax
from jax.experimental import pallas as pl
from jax.experimental.pallas import tpu as pltpu
from jax.sharding import Mesh
from jax.sharding import PartitionSpec as P

BF = jnp.bfloat16
F32 = jnp.float32
EPSILON = 1e-05
NEGATIVE = -1000000000.0
AXES = ("x", "y", "z", "c")
CHIPS = ("x", "y", "z")
ROWS = 256
PAIRS = 2
ALL = ROWS * PAIRS
D = 512
FF = 2048
VMEM = 61 * 1024 * 1024
ATTN_NORMS = (0, 2, 3)
FFN_NORMS = (1, 4)


def nn(a, b):
    return jnp.dot(a, b, preferred_element_type=F32)


def nt(a, b):
    return lax.dot_general(a, b, (((1,), (1,)), ((), ())), preferred_element_type=F32)


def tn(a, b):
    return lax.dot_general(a, b, (((0,), (0,)), ((), ())), preferred_element_type=F32)


def rows_of(b):
    return pl.ds(pl.multiple_of(b * ROWS, ROWS), ROWS)


def split_pair(stage, n, store_a, store_b):
    def body(i, carry):
        both = stage[n, pl.ds(pl.multiple_of(128 * i, 128), 128), :].astype(F32).reshape(8, 16, 512)
        rows = pl.ds(pl.multiple_of(64 * i, 64), 64)
        store_a(rows, both[:, :8].reshape(64, 512).astype(BF))
        store_b(rows, both[:, 8:].reshape(64, 512).astype(BF))
        return carry

    lax.fori_loop(0, 8, body, 0, unroll=8)


def prep_attn(stage, n, copies, dst):
    for half in range(2):
        copies[n + half].wait()

        def put(slot):
            def store(rows, value):
                dst[slot, rows, :] = value

            return store

        split_pair(stage, n + half, put(2 * half), put(2 * half + 1))


def prep_ffn(stage, n, copies, w_in, w_out):
    for half in range(2):
        copies[n + half].wait()

        def put(block):
            def store(rows, value):
                w_in[rows, 512 * block : 512 * block + 512] = value

            return store

        split_pair(stage, n + half, put(2 * half), put(2 * half + 1))
    copies[n + 2].wait()
    copies[n + 3].wait()

    def body(i, carry):
        span = pl.ds(pl.multiple_of(64 * i, 64), 64)
        first = stage[n + 2, span, :].astype(F32).reshape(4, 16, 512)
        second = stage[n + 3, span, :].astype(F32).reshape(4, 16, 512)
        whole = jnp.concatenate([first[:, :8], second[:, :8], first[:, 8:], second[:, 8:]], axis=1)
        w_out[pl.ds(pl.multiple_of(128 * i, 128), 128), :] = whole.reshape(128, 512).astype(BF)
        return carry

    lax.fori_loop(0, 16, body, 0, unroll=8)


def vector_kernel(block, vec, bin_vec):
    lines = block[...]
    turned = jnp.transpose(lines.astype(F32)).astype(BF)
    device = lax.broadcasted_iota(jnp.int32, (128, 512), 0)
    place = lax.broadcasted_iota(jnp.int32, (128, 512), 1)
    total = jnp.zeros((32, 512), F32)
    for e in range(4):
        spread = jnp.where(place == 4 * device + e, 1.0, 0.0).astype(BF)
        total = total + nn(turned[32 * e : 32 * e + 32], spread)
    vec[...] = total
    bin_vec[...] = jnp.zeros_like(bin_vec)
    for k in range(4):
        near_by = jnp.where((place + 512 * k) // 16 == device, 1.0, 0.0)
        for j in range(2):
            pick = jnp.where(device == 32 * (place % 4) + 24 + 4 * j + (place % 16) // 4, 1.0, 0.0)
            found = nn(lines, pick.astype(BF)) * near_by
            bin_vec[j : j + 1, 512 * k : 512 * k + 512] = jnp.sum(found, 0, keepdims=True)


def norm_forward(r, gain, shift):
    c = r - jnp.mean(r, -1, keepdims=True)
    inv = lax.rsqrt(jnp.mean(c * c, -1, keepdims=True) + EPSILON)
    xhat = c * inv
    return xhat * gain + shift, xhat, inv


def norm_backward(g, xhat, inv, gain):
    d_gain = jnp.sum(g * xhat, 0, keepdims=True)
    d_shift = jnp.sum(g, 0, keepdims=True)
    gs = g * gain
    dr = inv * (gs - jnp.mean(gs, -1, keepdims=True) - xhat * jnp.mean(gs * xhat, -1, keepdims=True))
    return dr, d_gain, d_shift


def low_half():
    return lax.broadcasted_iota(jnp.int32, (1, 128), 1) < 64


def blocks(size, total, body):
    def step(i, carry):
        body(pl.ds(pl.multiple_of(i * size, size), size))
        return carry

    lax.fori_loop(0, total // size, step, 0, unroll=8)


def attn_forward(x, h, m, w, biases, mask_of, q_ref, k_ref, v_ref, o_ref, e_ref, r_ref, after):
    for n in range(2):
        cols = pl.ds(256 * n, 256)
        part = slice(256 * n, 256 * n + 256)
        q_ref[:, cols] = ((nn(h[...], w[0, :, cols]) + biases[0][:, part]) * 0.125).astype(BF)
        k_ref[:, cols] = nn(m[...], w[1, :, cols]).astype(BF)
        v_ref[:, cols] = (nn(m[...], w[2, :, cols]) + biases[1][:, part]).astype(BF)
    low = low_half()

    def pair(b, carry):
        rows = rows_of(b)
        masked = mask_of(b)
        for j in range(4):
            cols = pl.ds(128 * j, 128)
            q = q_ref[rows, cols]
            k = k_ref[rows, cols]
            v = jnp.concatenate([v_ref[rows, cols], jnp.ones((ROWS, 128), BF)], axis=1)
            parts = []
            for half in range(2):
                mine = low if half == 0 else jnp.logical_not(low)
                s = nt(jnp.where(mine, q, jnp.zeros_like(q)), k) + masked
                e = jnp.exp(s - jnp.max(s, -1, keepdims=True)).astype(BF)
                e_ref[8 * b + 2 * j + half] = e
                parts.append(nn(e, v))
            r = 1.0 / jnp.where(low, parts[0][:, 128:], parts[1][:, 128:])
            r_ref[rows, cols] = r.astype(BF)
            o = jnp.where(low, parts[0][:, :128], parts[1][:, :128]) * r
            o_ref[rows, cols] = o.astype(BF)
        after(rows, b, x(rows) + (nn(o_ref[rows, :], w[3]) + biases[2]))
        return carry

    lax.fori_loop(0, PAIRS, pair, 0, unroll=True)


def attn_backward(b, d_o, q_ref, k_ref, v_ref, o_ref, e_ref, r_ref, dq_ref, dk_ref, dv_ref):
    rows = rows_of(b)
    low = low_half()
    for j in range(4):
        cols = pl.ds(128 * j, 128)
        q = q_ref[rows, cols]
        k = k_ref[rows, cols]
        v = v_ref[rows, cols]
        ds_o = d_o[rows, cols].astype(F32) * r_ref[rows, cols].astype(F32)
        prod = ds_o * o_ref[rows, cols].astype(F32)
        ds_o = ds_o.astype(BF)
        dqs, dks, dvs = [], [], []
        for half in range(2):
            mine = low if half == 0 else jnp.logical_not(low)
            delta = jnp.sum(jnp.where(mine, prod, 0.0), -1, keepdims=True)
            e = e_ref[8 * b + 2 * j + half]
            dp = nt(jnp.where(mine, ds_o, jnp.zeros_like(ds_o)), v)
            ds = (e.astype(F32) * (dp - delta)).astype(BF)
            dvs.append(tn(e, ds_o))
            dqs.append(nn(ds, k))
            dks.append(tn(ds, q))
        dq_ref[rows, cols] = (jnp.where(low, dqs[0], dqs[1]) * 0.125).astype(BF)
        dk_ref[rows, cols] = jnp.where(low, dks[0], dks[1]).astype(BF)
        dv_ref[rows, cols] = jnp.where(low, dvs[0], dvs[1]).astype(BF)


def gelu_both(u):
    c = 0.7978845608028654
    square = u * u
    t = jnp.tanh(c * u * (1.0 + 0.044715 * square))
    half = 0.5 * (1.0 + t)
    act = u * half
    slope = half + (0.5 * c) * u * (1.0 - t * t) * (1.0 + (3.0 * 0.044715) * square)
    return act, slope


def ffn_forward(x, h, w_in, w_out, b_in, b_out, act_ref, slope_ref, after):
    def hidden(cols):
        act, slope = gelu_both(nn(h[...], w_in[:, cols]) + b_in[:, cols])
        act_ref[:, cols] = act.astype(BF)
        slope_ref[:, cols] = slope.astype(BF)

    blocks(256, FF, hidden)

    def pair(b, carry):
        rows = rows_of(b)
        after(rows, b, x(rows) + (nn(act_ref[rows, :], w_out[...]) + b_out))
        return carry

    lax.fori_loop(0, PAIRS, pair, 0, unroll=True)


def ffn_backward(dr, df, w_in, w_out, slope_ref, du_ref, bin_grad, dx):
    def hidden(cols):
        du = nt(df[...], w_out[cols, :]) * slope_ref[:, cols].astype(F32)
        bin_grad[0:1, cols] = jnp.sum(du, 0, keepdims=True)
        du_ref[:, cols] = du.astype(BF)

    blocks(256, FF, hidden)

    def pair(b, carry):
        rows = rows_of(b)
        dx[rows, :] = dr[rows, :] + nt(du_ref[rows, :], w_in[...])
        return carry

    lax.fori_loop(0, PAIRS, pair, 0, unroll=True)


def turn(src, cols, dst):
    dst[...] = jnp.transpose(src[:, cols])


def ffn_weight_grads(h_ref, du_ref, act_ref, df_ref, g, turned, base, inner_done):
    turn(h_ref, slice(None), turned)

    def inner(k, carry):
        for n in range(2):
            part = nn(turned[...], du_ref[:, pl.ds(pl.multiple_of(512 * k + 256 * n, 256), 256)])
            at = pl.ds(pl.multiple_of(base + 512 * (k // 2) + 256 * n, 256), 256)
            g[k % 2, :, at] = part.astype(BF)
        return carry

    lax.fori_loop(0, 4, inner, 0, unroll=True)
    inner_done()

    def outer(j, carry):
        turn(act_ref, pl.ds(pl.multiple_of(512 * j, 512), 512), turned)
        rows = pl.ds(pl.multiple_of(128 * j, 128), 128)
        for n in range(2):
            part = nn(turned[...], df_ref[:, 256 * n : 256 * n + 256]).reshape(16, 4, 8, 256)
            for k in range(4):
                at = base + 1024 + 512 * (k % 2) + 256 * n
                g[k // 2, rows, at : at + 256] = part[:, k].reshape(128, 256).astype(BF)
        return carry

    lax.fori_loop(0, 4, outer, 0, unroll=4)


def planes_first(part):
    wide = part.shape[-1]
    return part.reshape(4, 16, 8, wide).transpose(1, 0, 2, 3).reshape(512, wide)


def attn_weight_grads(h_ref, m_ref, o_ref, da_ref, dq_ref, dk_ref, dv_ref, g, turned, base, order):
    def product(side, at, right):
        for n in range(2):
            cols = slice(256 * n, 256 * n + 256)
            start = base + at + 256 * n
            g[side, :, start : start + 256] = order(nn(turned[...], right[:, cols])).astype(BF)

    turn(h_ref, slice(None), turned)
    product(0, 0, dq_ref)
    if m_ref is not h_ref:
        turn(m_ref, slice(None), turned)
    product(1, 0, dk_ref)
    product(0, 512, dv_ref)
    turn(o_ref, slice(None), turned)
    product(1, 512, da_ref)


def send_out(g, core, mine, theirs, sems):
    other = pltpu.make_async_copy(g.at[1 - core], theirs, sems.at[0])
    own = pltpu.make_async_copy(g.at[core], mine, sems.at[1])
    other.start()
    own.start()
    return other, own


class Moves:
    def __init__(self, sems):
        self.sems, self.used, self.open = sems, 0, []

    def start(self, src, dst):
        copy = pltpu.make_async_copy(src, dst, self.sems.at[self.used])
        self.used += 1
        copy.start()
        return copy

    def send(self, src, dst):
        self.open.append(self.start(src, dst))

    def finish(self):
        for copy in self.open:
            copy.wait()


def fetch_pair(moves, gathered, stage, pair, slot):
    return moves.start(gathered.at[:, pl.ds(512 * pair, 512)], stage.at[slot])


def forward_kernel(scalars, gathered, vec, bin_vec, src_h, tgt_h, og_h, *refs):
    (
        dec_h, grad_h,
        q0h, k0h, v0h, o0h, e0h, r0h, q1h, k1h, v1h, o1h, e1h, r1h, q2h, k2h, v2h, o2h, e2h, r2h,
        xh0h, xh1h, xh2h, xh3h, inv0h, inv1h, inv2h, inv3h,
        enc_h, mem_h, first_h, act0h, slope0h, mine, theirs, vec_grad, bin_grad,
        dec, grad_d2,
        q0, k0, v0, o0, e0, r0, q1, k1, v1, o1, e1, r1, q2, k2, v2, o2, e2, r2,
        xh0, xh1, xh2, xh3, inv0, inv1, inv2, inv3,
        enc, mem, first, act0, slope0,
        src, tgt, og, stage, w_attn, w_in, w_out, x32, second,
        act1, slope1, df, g, turned, sems,
    ) = refs
    moves = Moves(sems)
    pairs = {n: fetch_pair(moves, gathered, stage, n, n) for n in (0, 1)}
    src_in = moves.start(src_h, src)

    def bias(layer):
        return [vec[3 * layer + j : 3 * layer + j + 1, :] for j in range(3)]

    def gain(n):
        return vec[9 + n : 10 + n, :]

    def shift(n):
        return vec[14 + n : 15 + n, :]

    def source_keys(b):
        place = lax.broadcasted_iota(jnp.int32, (1, ROWS), 1)
        return jnp.where(place < scalars[b], 0.0, NEGATIVE)

    def target_keys(b):
        at_q = lax.broadcasted_iota(jnp.int32, (ROWS, ROWS), 0)
        at_k = lax.broadcasted_iota(jnp.int32, (ROWS, ROWS), 1)
        live = jnp.logical_and(at_q >= at_k, at_k < scalars[2 + b])
        return jnp.where(live, 0.0, NEGATIVE)

    def keeper(n, xh, inv_ref, low, wide):
        def after(rows, b, r):
            z, xhat, inv = norm_forward(r, gain(n), shift(n))
            xh[rows, :] = xhat.astype(BF)
            inv_ref[rows, :] = jnp.broadcast_to(inv, (ROWS, 128))
            low[rows, :] = z.astype(BF)
            if wide is not None:
                wide[rows, :] = z

        return after

    def from_low(ref):
        return lambda rows: ref[rows, :].astype(F32)

    def from_x32(rows):
        return x32[rows, :]

    src_in.wait()
    prep_attn(stage, 0, [pairs[0], pairs[1]], w_attn)
    for n in range(4):
        pairs[6 + n] = fetch_pair(moves, gathered, stage, 6 + n, 2 + n)
    tgt_in = moves.start(tgt_h, tgt)
    for n in (2, 3):
        pairs[n] = fetch_pair(moves, gathered, stage, n, 4 + n)
    og_in = moves.start(og_h, og)
    pairs[4] = fetch_pair(moves, gathered, stage, 4, 0)
    pairs[5] = fetch_pair(moves, gathered, stage, 5, 1)
    attn_forward(
        from_low(src), src, src, w_attn, bias(0), source_keys, q0, k0, v0, o0, e0, r0,
        keeper(0, xh0, inv0, enc, x32),
    )
    for a, b in ((q0, q0h), (k0, k0h), (v0, v0h), (o0, o0h), (e0, e0h), (r0, r0h),
                 (xh0, xh0h), (inv0, inv0h), (enc, enc_h)):
        moves.send(a, b)
    prep_ffn(stage, 2, [None, None] + [pairs[6 + n] for n in range(4)], w_in, w_out)
    for n in range(4):
        pairs[10 + n] = fetch_pair(moves, gathered, stage, 10 + n, 2 + n)
    ffn_forward(
        from_x32, enc, w_in, w_out, bin_vec.at[0:1], vec[19:20, :], act0, slope0,
        keeper(1, xh1, inv1, mem, None),
    )
    for a, b in ((xh1, xh1h), (inv1, inv1h), (mem, mem_h), (act0, act0h), (slope0, slope0h)):
        moves.send(a, b)
    tgt_in.wait()
    prep_attn(stage, 6, [None] * 6 + [pairs[2], pairs[3]], w_attn)
    attn_forward(
        from_low(tgt), tgt, tgt, w_attn, bias(1), target_keys, q1, k1, v1, o1, e1, r1,
        keeper(2, xh2, inv2, first, x32),
    )
    for a, b in ((q1, q1h), (k1, k1h), (v1, v1h), (o1, o1h), (e1, e1h), (r1, r1h),
                 (xh2, xh2h), (inv2, inv2h), (first, first_h)):
        moves.send(a, b)
    prep_attn(stage, 0, [pairs[4], pairs[5]], w_attn)
    attn_forward(
        from_x32, first, mem, w_attn, bias(2), source_keys, q2, k2, v2, o2, e2, r2,
        keeper(3, xh3, inv3, second, x32),
    )
    for a, b in ((q2, q2h), (k2, k2h), (v2, v2h), (o2, o2h), (e2, e2h), (r2, r2h),
                 (xh3, xh3h), (inv3, inv3h)):
        moves.send(a, b)
    prep_ffn(stage, 2, [None, None] + [pairs[10 + n] for n in range(4)], w_in, w_out)
    vec_grad[...] = jnp.zeros_like(vec_grad)
    bin_grad[...] = jnp.zeros_like(bin_grad)
    og_in.wait()

    def last(rows, b, r):
        z, xhat, inv = norm_forward(r, gain(4), shift(4))
        dec[rows, :] = z.astype(BF)
        at = lax.broadcasted_iota(jnp.int32, (ROWS, 1), 0)
        gz = jnp.where(at < scalars[2 + b], og[rows, :].astype(F32), 0.0)
        dr, d_gain, d_shift = norm_backward(gz, xhat, inv, gain(4))
        vec_grad[0:1, :] += d_gain
        vec_grad[1:2, :] += d_shift
        vec_grad[2:3, :] += jnp.sum(dr, 0, keepdims=True)
        df[rows, :] = dr.astype(BF)
        x32[rows, :] = dr

    ffn_forward(
        from_x32, second, w_in, w_out, bin_vec.at[1:2], vec[20:21, :], act1, slope1, last
    )
    moves.send(dec, dec_h)
    ffn_backward(x32, df, w_in, w_out, slope1, slope1, bin_grad, grad_d2)
    moves.send(grad_d2, grad_h)
    core = scalars[4]

    def inner_done():
        send_gradients(moves, g, core, mine, theirs, 0, 1024)

    ffn_weight_grads(second, slope1, act1, df, g, turned, 0, inner_done)
    send_gradients(moves, g, core, mine, theirs, 1024, 1024)
    moves.finish()


def norm_rows(vec_grad, grad, xh, inv, gain, low, wide):
    vec_grad[...] = jnp.zeros_like(vec_grad)

    def pair(b, carry):
        rows = rows_of(b)
        dr, d_gain, d_shift = norm_backward(
            grad[rows, :], xh[rows, :].astype(F32), inv[rows, 0:1], gain
        )
        vec_grad[0:1, :] += d_gain
        vec_grad[1:2, :] += d_shift
        vec_grad[2:3, :] += jnp.sum(dr, 0, keepdims=True)
        low[rows, :] = dr.astype(BF)
        wide[rows, :] = dr
        return carry

    lax.fori_loop(0, PAIRS, pair, 0, unroll=True)


def load_attn(moves, far_refs, near_refs):
    far_refs, near_refs = list(far_refs), list(near_refs)
    first = [moves.start(a, b) for a, b in zip(far_refs[:2], near_refs[:2])]
    heads = [moves.start(a, b) for a, b in zip(far_refs[2:8], near_refs[2:8])]
    rows = [moves.start(a, b) for a, b in zip(far_refs[8:], near_refs[8:])]
    return first, heads, rows


def attn_back(grad, data, weights, w, gain, temps, dx, grad_mem, g, base, vec_grad, copies, arrived, order):
    xh, inv, r, o, q, v, k, e, h = data[:9]
    m = data[9] if len(data) > 9 else h
    da, d_o, dq, dk, dv, turned = temps
    first, heads, rows_in = copies
    for copy in first:
        copy.wait()
    norm_rows(vec_grad, grad, xh, inv, gain, da, dx)
    weights()
    for n in range(2):
        cols = pl.ds(256 * n, 256)
        d_o[:, cols] = nt(da[...], w[3, cols, :]).astype(BF)
    for copy in heads:
        copy.wait()
    arrived()

    def body(b, carry):
        attn_backward(b, d_o, q, k, v, o, e, r, dq, dk, dv)
        rows = rows_of(b)
        vec_grad[3:4, :] += jnp.sum(dq[rows, :].astype(F32), 0, keepdims=True)
        vec_grad[4:5, :] += jnp.sum(dv[rows, :].astype(F32), 0, keepdims=True)
        to_m = nt(dk[rows, :], w[1]) + nt(dv[rows, :], w[2])
        to_x = dx[rows, :] + nt(dq[rows, :], w[0])
        if grad_mem is not None:
            grad_mem[rows, :] = to_m
            dx[rows, :] = to_x
        else:
            dx[rows, :] = to_x + to_m
        return carry

    lax.fori_loop(0, PAIRS, body, 0, unroll=True)
    for copy in rows_in:
        copy.wait()
    attn_weight_grads(h, m, o, da, dq, dk, dv, g, turned, base, order)


def send_gradients(moves, g, core, mine, theirs, at, size):
    cols = pl.ds(at, size)
    moves.send(g.at[1 - core, :, cols], theirs.at[:, cols])
    moves.send(g.at[core, :, cols], mine.at[:, cols])


def middle_kernel(scalars, gathered, vec, grad_h, *refs):
    far_attn, far_ffn = refs[:10], refs[10:15]
    d1_h, denc_h, mine, theirs, attn_vec, ffn_vec, bin_grad = refs[15:22]
    near_attn, near_ffn = refs[22:32], refs[32:37]
    grad, d1, denc, stage, w, w_in, w_out, da, d_o, dq, dk, dv, g, turned, sems = refs[37:]
    moves = Moves(sems)
    grad_in = moves.start(grad_h, grad)
    pairs = [fetch_pair(moves, gathered, stage, 4 + n, n) for n in range(2)]
    copies = load_attn(moves, far_attn, near_attn)
    xh1, inv1, slope, act, enc = near_ffn
    ffn_in = []

    def arrived():
        pairs.extend([fetch_pair(moves, gathered, stage, 6 + n, 2 + n) for n in range(4)])
        ffn_in.extend([moves.start(a, b) for a, b in zip(far_ffn, near_ffn)])

    bin_grad[...] = jnp.zeros_like(bin_grad)
    grad_in.wait()
    attn_back(
        grad, near_attn, lambda: prep_attn(stage, 0, pairs, w), w, vec[12:13, :],
        (da, d_o, dq, dk, dv, turned), d1, grad, g, 0, attn_vec, copies, arrived, lambda part: part,
    )
    core = scalars[4]
    send_gradients(moves, g, core, mine, theirs, 0, 1024)
    moves.send(d1, d1_h)
    for copy in ffn_in:
        copy.wait()
    norm_rows(ffn_vec, grad, xh1, inv1, vec[10:11, :], da, grad)
    prep_ffn(stage, 2, [None, None] + pairs[2:], w_in, w_out)
    ffn_backward(grad, da, w_in, w_out, slope, slope, bin_grad, denc)
    moves.send(denc, denc_h)

    def inner_done():
        send_gradients(moves, g, core, mine, theirs, 1024, 1024)

    ffn_weight_grads(enc, slope, act, da, g, turned, 1024, inner_done)
    send_gradients(moves, g, core, mine, theirs, 2048, 1024)
    moves.finish()


def write_vectors(attn, ffn, ffn_bins, g, at):
    rows = [attn[i][r : r + 1, :] for i in range(3) for r in (3, 4, 2)]
    order = (attn[0], ffn[0], attn[1], attn[2], ffn[1])
    rows += [a[0:1, :] for a in order] + [a[1:2, :] for a in order] + [f[2:3, :] for f in ffn]
    whole = jnp.concatenate(rows + [jnp.zeros((3, 512), F32)], axis=0)
    wide = jnp.concatenate([f[0:1, :] for f in ffn_bins] + [jnp.zeros((6, FF), F32)], axis=0)
    lane = lax.broadcasted_iota(jnp.int32, (8, 128), 1)
    tiles = []
    for p in [16 * x + yz for yz in range(16) for x in range(4)]:
        cols = slice(128 * (p // 16), 128 * (p // 16) + 128)
        tile = jnp.zeros((8, 128), F32)
        for n in range(3):
            turned = pltpu.roll(whole[8 * n : 8 * n + 8, cols], (8 * n - 8 * (p % 16)) % 128, 1)
            tile = jnp.where(lane // 8 == n, turned, tile)
        cols = slice(128 * (p // 4), 128 * (p // 4) + 128)
        turned = pltpu.roll(wide[:, cols], (32 - 32 * (p % 4)) % 128, 1)
        tiles.append(jnp.where(lane // 32 == 1, turned, tile))
    block = jnp.concatenate(tiles, axis=0).astype(BF)
    for side in range(2):
        g[side, :, at : at + 128] = block


def last_kernel(scalars, gathered, vec, a2_vec, f0_vec, f1_vec, f0_bin, f1_bin, *refs):
    far_data = [refs[10 * i : 10 * i + 10] for i in range(2)]
    dx_h, (mine, theirs) = refs[20:22], refs[22:24]
    near_data = [refs[24 + 10 * i : 34 + 10 * i] for i in range(2)]
    dx, vec_grad = refs[44:46], refs[46:48]
    stage, w, da, d_o, dq, dk, dv, g, turned, sems = refs[48:]
    moves = Moves(sems)
    grads, pairs, copies = [], [], []
    core = scalars[4]

    def start():
        i = len(grads)
        if i < 2:
            grads.append(moves.start(far_data[i][0], near_data[i][0]))
            slots = range(2 * i, 2 * i + 2)
            pairs.extend([fetch_pair(moves, gathered, stage, n, n) for n in slots])
            copies.append(load_attn(moves, far_data[i][1:], near_data[i][1:]))

    start()
    for i in range(2):
        norm = 9 + ATTN_NORMS[i]
        grads[i].wait()
        attn_back(
            near_data[i][0], near_data[i][1:], lambda: prep_attn(stage, 2 * i, pairs, w), w,
            vec[norm : norm + 1, :], (da, d_o, dq, dk, dv, turned), dx[i], None, g, 1024 * i,
            vec_grad[i], copies[i], start, planes_first,
        )
        if i == 1:
            write_vectors((*vec_grad, a2_vec), (f0_vec, f1_vec), (f0_bin, f1_bin), g, 2048)
        send_gradients(moves, g, core, mine, theirs, 1024 * i, 1024 + 128 * i)
        moves.send(dx[i], dx_h[i])
    moves.finish()


def spec(space):
    return pl.BlockSpec(memory_space=space)


def call(kernel, name, inputs, outs, scratch, after=()):
    taken = len(inputs)
    inputs = inputs + [(a, H) for a in after]

    def body(*refs):
        kernel(*refs[:taken], *refs[len(inputs) :])

    return pl.pallas_call(
        body,
        name=name,
        in_specs=[spec(s) for _, s in inputs],
        out_specs=[spec(s) for _, _, s in outs],
        out_shape=[jax.ShapeDtypeStruct(shape, kind) for shape, kind, _ in outs],
        scratch_shapes=scratch,
        compiler_params=pltpu.CompilerParams(vmem_limit_bytes=VMEM),
        cost_estimate=pl.CostEstimate(flops=10**10, bytes_accessed=10**7, transcendentals=0),
    )(*[a for a, _ in inputs])


V, H, S = pltpu.VMEM, pl.ANY, pltpu.SMEM
ROW = ((ALL, D), BF)
WIDE = ((ALL, FF), BF)
LINE = ((ALL, D), F32)
INV = ((ALL, 128), F32)
EXP = ((8 * PAIRS, ROWS, ROWS), BF)
VEC = ((8, D), F32, V)
BIN = ((8, FF), F32, V)


def far(kinds):
    return [(shape, kind, H) for shape, kind in kinds]


def near(kinds):
    return [V(shape, kind) for shape, kind in kinds]


def run_vectors(block):
    return call(vector_kernel, "vectors", [(block, V)], [((32, D), F32, V), BIN], [])


def run_forward(scalars, gathered, vec, bin_vec, src, tgt, og):
    kept = (
        [ROW, LINE] + [ROW, ROW, ROW, ROW, EXP, ROW] * 3 + [ROW] * 4 + [INV] * 4
        + [ROW] * 3 + [WIDE, WIDE]
    )
    outs = far(kept) + [((D, FF), BF, H)] * 2 + [VEC, BIN]
    scratch = near(kept) + near([ROW, ROW, ROW]) + [
        V((8, 1024, 512), BF), V((4, 512, 512), BF),
        V((D, FF), BF), V((FF, D), BF), V((ALL, D), F32), V((ALL, D), BF),
        V((ALL, FF), BF), V((ALL, FF), BF), V((ALL, D), BF),
        V((2, D, FF), BF), V((D, ALL), BF), pltpu.SemaphoreType.DMA((64,)),
    ]
    return call(
        forward_kernel, "forward",
        [(scalars, S), (gathered, H), (vec, V), (bin_vec, V), (src, H), (tgt, H), (og, H)], outs, scratch,
    )


ATTN_DATA = [ROW, INV, ROW, ROW, ROW, ROW, ROW, EXP, ROW]


def attn_data(xh, inv, heads, *rows):
    q, k, v, o, e, r = heads
    return [xh, inv, r, o, q, v, k, e, *rows]


def run_middle(scalars, gathered, vec, grad, attn, ffn, after=()):
    kinds = ATTN_DATA + [ROW] + [ROW, INV, WIDE, WIDE, ROW]
    inputs = [(scalars, S), (gathered, H), (vec, V)] + [(a, H) for a in (grad, *attn, *ffn)]
    outs = far([LINE, LINE]) + [((D, 3072), BF, H)] * 2 + [VEC, VEC, BIN]
    scratch = near(kinds) + near([LINE] * 3) + [
        V((6, 1024, 512), BF), V((4, 512, 512), BF), V((D, FF), BF), V((FF, D), BF),
        *near([ROW] * 5), V((2, D, 3072), BF), V((D, ALL), BF), pltpu.SemaphoreType.DMA((40,)),
    ]
    return call(middle_kernel, "middle", inputs, outs, scratch, after)


def run_last(scalars, gathered, vec, sums, data, after=()):
    kinds = ([LINE] + ATTN_DATA) * 2
    inputs = [(scalars, S), (gathered, H), (vec, V)]
    inputs += [(a, V) for a in sums] + [(a, H) for a in data]
    outs = far([LINE, LINE]) + [((D, 2176), BF, H)] * 2
    scratch = near(kinds) + near([LINE] * 2) + [V((8, D), F32), V((8, D), F32)] + [
        V((4, 1024, 512), BF), V((4, 512, 512), BF), *near([ROW] * 5), V((2, D, 2176), BF),
        V((D, ALL), BF), pltpu.SemaphoreType.DMA((40,)),
    ]
    return call(last_kernel, "last", inputs, outs, scratch, after)


def pack_shard(c, attn_proj, attn_out, attn_bias, norm_gain, norm_shift, ffn_in, ffn_out, b_in, b_out):
    attn = jnp.concatenate([attn_proj, attn_out[:, None]], axis=1).reshape(12, 4, 512)
    wide = ffn_in.reshape(2, 4, 4, 512).transpose(0, 2, 1, 3).reshape(8, 4, 512)
    both = lax.all_gather(jnp.concatenate([attn, wide]), "c", axis=1, tiled=True)
    half = lax.dynamic_index_in_dim(both.reshape(10, 2, 8, 512), c, 1, False)
    tall = ffn_out.reshape(2, 2, 8, 512)
    blocks = jnp.concatenate([half[:8], tall[0], half[8:], tall[1]])
    vec = [attn_bias.reshape(9, 4), norm_gain, norm_shift, b_out, jnp.zeros((3, 4), BF)]
    line = jnp.concatenate(vec + [b_in.reshape(8, 4)]).T.reshape(1, 128)
    return blocks.transpose(1, 0, 2).reshape(8, 7168), line


def swap(a):
    return lax.ppermute(a, "c", [(0, 1), (1, 0)])


def pair_sum(mine, theirs):
    return (mine.astype(F32) + swap(theirs).astype(F32)).astype(BF)


def ring_sum(whole):
    return lax.psum_scatter(whole, "x", scatter_dimension=0, tiled=True)


def plane_sum(whole):
    whole = whole.reshape(16, -1, whole.shape[1])
    whole = lax.all_to_all(whole, ("y", "z"), 0, 0, tiled=True)
    return jnp.sum(whole.astype(F32), axis=0)


def line_sum(whole):
    blocks = whole.reshape(4, 8, -1)
    x = lax.axis_index("x")
    total = lax.dynamic_index_in_dim(blocks, x, 0, False)
    for k in range(1, 4):
        part = lax.dynamic_index_in_dim(blocks, (x + k) % 4, 0, False).astype(BF)
        part = lax.ppermute(part, "x", [(i, (i + k) % 4) for i in range(4)])
        total = total + part.astype(F32)
    return total


def per_device(source, target, src_len, tgt_len, out_grad, *weights):
    c = lax.axis_index("c")
    shard, line = pack_shard(c, *weights)
    gathered = lax.all_gather(shard, AXES, axis=0, tiled=True)
    vec, bin_vec = run_vectors(lax.all_gather(line, AXES, axis=0, tiled=True))
    scalars = jnp.concatenate(
        [src_len.reshape(2), tgt_len.reshape(2), c.astype(jnp.int32)[None], jnp.zeros(3, jnp.int32)]
    )
    src, tgt, og = (a.reshape(ALL, D) for a in (source, target, out_grad))
    outs = run_forward(scalars, gathered, vec, bin_vec, src, tgt, og)
    dec, grad = outs[:2]
    heads = [outs[2 + 6 * i : 8 + 6 * i] for i in range(3)]
    xh, inv = outs[20:24], outs[24:28]
    enc, mem, first, act0, slope0, f1_mine, f1_theirs, f1_vec, f1_bin = outs[28:]
    f1 = pair_sum(f1_mine, f1_theirs)
    f1_x = ring_sum(f1)
    d1, d_enc, mid_mine, mid_theirs, a2_vec, f0_vec, f0_bin = run_middle(
        scalars, gathered, vec, grad, attn_data(xh[3], inv[3], heads[2], first, mem),
        [xh[1], inv[1], slope0, act0, enc], (f1,),
    )
    mid = pair_sum(mid_mine, mid_theirs)
    mid_x = ring_sum(mid)
    data = [d_enc, *attn_data(xh[0], inv[0], heads[0], src)]
    data += [d1, *attn_data(xh[2], inv[2], heads[1], tgt)]
    d_src, d_tgt, end_mine, end_theirs = run_last(
        scalars, gathered, vec, (a2_vec, f0_vec, f1_vec, f0_bin, f1_bin), data, (mid, f1_x)
    )
    end = plane_sum(pair_sum(end_mine, end_theirs))
    mid_x, end = lax.optimization_barrier((mid_x, end))
    sum_end = line_sum(end)
    sum_rest = plane_sum(jnp.concatenate([mid_x, f1_x], axis=1))

    cut = sum_end[:, 2048:]
    vecs = cut[:, :24].reshape(8, 3, 2, 4).transpose(1, 0, 2, 3).reshape(24, 2, 4)
    vecs = lax.dynamic_index_in_dim(vecs, c, 1, False)
    g_bin = lax.dynamic_index_in_dim(cut[:2, 32:64].reshape(2, 2, 16), c, 1, False)
    whole = jnp.concatenate([sum_end[:, :2048], sum_rest], axis=1)
    attn = whole[:, :3072].reshape(2, 4, 6, 512)
    wide = whole[:, 3072:].reshape(8, 2, 4, 512)
    rows = jnp.concatenate([attn, wide[:, :, :2].reshape(2, 4, 4, 512)], axis=2)
    keep = lax.dynamic_index_in_dim(rows, c, 0, False)
    got = swap(lax.dynamic_index_in_dim(rows, 1 - c, 0, False))
    first_half = jnp.where(c == 0, keep, got)
    second_half = jnp.where(c == 0, got, keep)
    a = first_half[:, :6].reshape(4, 3, 2, 512)
    b = second_half[:, :6].reshape(4, 3, 2, 512)
    g_proj = jnp.stack([a[:, :, 0], b[:, :, 0], a[:, :, 1]], axis=0).transpose(2, 0, 1, 3)
    g_out = b[:, :, 1].transpose(1, 0, 2)
    ia = first_half[:, 6:].reshape(4, 2, 2, 512)
    ib = second_half[:, 6:].reshape(4, 2, 2, 512)
    g_in = jnp.stack([ia, ib], axis=3).transpose(1, 0, 2, 3, 4).reshape(2, 4, 2048)
    g_wout = wide[:, :, 2:].transpose(1, 2, 0, 3).reshape(2, 16, 512)
    shape = source.shape
    return (
        dec.reshape(shape), d_src.reshape(shape), d_tgt.reshape(shape),
        g_proj, g_out, vecs[:9].reshape(3, 3, 4), vecs[9:14], vecs[14:19],
        g_in, g_wout, g_bin, vecs[19:21],
    )


def solution(mesh):
    mesh = Mesh(mesh.devices.reshape(4, 4, 4, 2), AXES)
    rows = P(None, AXES, None, None)
    lens = P(None, AXES)
    weights = (
        P(None, None, AXES, None), P(None, AXES, None), P(None, None, AXES), P(None, AXES),
        P(None, AXES), P(None, AXES, None), P(None, AXES, None), P(None, AXES), P(None, AXES),
    )
    return jax.shard_map(
        per_device,
        mesh=mesh,
        in_specs=(rows, rows, lens, lens, rows) + weights,
        out_specs=(rows, rows, rows) + weights,
        check_vma=False,
    )
```

profile of v0, /device:TPU:1, one launch (start us, length us, event | category | flops | bytes accessed | tf_op | source)
XLA Modules:
  0.0 267.4 jit_solution(4325441406160739105)
XLA Ops:
  7.2 0.8 fusion.7
  8.0 0.8 pad_maximum_fusion.3
  9.0 3.0 %all_gather.9 = bf16[20,8,512]{2,0,1:T(8,128)(2,1)S(1)} all-gather(bf16[20,4,512]{2,0,1:T(8,128)(2,1)S(1)} %copy.99), channel_id=1, replica_groups=mesh['x'=4,'y'=4,'z'=4,'c'=2] {'c'}, dimensions={1}, use_global_device_ids=true | all-gather | bytes 245760 | tf_op jit(solution)/shard_map/all_gather | solution.py:712
  12.1 0.7 slice_bitcast_fusion.6
  13.6 0.7 reshape.159
  14.4 0.7 reshape.134
  15.2 0.8 copy.102
  16.0 0.8 concatenate.32
  16.8 33.3 %all-gather = bf16[128,1,128]{2,1,0:T(2,128)(2,1)S(1)} all-gather(bf16[1,1,128]{2,1,0:T(2,128)(2,1)S(1)} %reshape.156), channel_id=1, replica_groups=mesh['x'=4,'y'=4,'z'=4,'c'=2] {'x','y','z','c'}, dimensions={0}, use_global_device_ids=true | all-gather | bytes 33024 | tf_op jit(solution)/shard_map/all_gather | solution.py:754
  50.7 1.3 pad_add_fusion.refs_0_
  52.0 1.9 vectors.1
  53.9 39.5 %all-gather.3.cloned.1.call-done.refs_1_ = bf16[1024,7168]{1,0:T(8,128)(2,1)} async-done(((bf16[8,7168]{1,0:T(8,128)(2,1)}), bf16[1024,7168]{1,0:T(8,128)(2,1)}) %all-gather.3.cloned.1.call-update) | async-done | bytes 14680080 | tf_op jit(solution)/shard_map/all_gather | solution.py:753
  93.3 32.2 %forward.1 = (bf16[512,512]{1,0:T(8,128)(2,1)}, f32[512,512]{1,0:T(8,128)}, bf16[512,512]{1,0:T(8,128)(2,1)}, bf16[512,512]{1,0:T(8,128)(2,1)}, bf16[512,512]{1,...) custom-call(s32[8]{0:T(128)} %pad_add_fusion.refs_0_, ...), custom_call_target="tpu_custom_call" | custom-call | flops 10000000000 | bytes 10000000 | tf_op jit(solution)/shard_map/forward/pallas_call | solution.py:626
  125.8 4.1 %collective-permute-done = bf16[512,2048]{1,0:T(8,128)(2,1)S(1)} collective-permute-done((bf16[512,2048]{1,0:T(8,128)(2,1)}, bf16[512,2048]{1,0:T(8,128)(2,1)S(1)}, u32[]{:S(2)}, u32[]{:S(2)}) %collective-permute-start) | collective-permute-done | bytes 2097184 | tf_op jit(solution)/shard_map/ppermute | solution.py:722
  129.9 3.7 %add_convert_fusion.2.refs_19_ = bf16[512,2048]{1,0:T(8,128)(2,1)} fusion(bf16[512,2048]{1,0:T(8,128)(2,1)S(1)} %collective-permute-done, bf16[512,2048]{1,0:T(8,128)(2,1)} %get-tuple-element.83), kind=kLoop, calls=%fused_computation.3 | loop fusion | flops 4194304 | bytes 6291456 | tf_op jit(solution)/shard_map/convert_element_type | solution.py:726
  133.9 17.8 %middle.1 = (f32[512,512]{1,0:T(8,128)}, f32[512,512]{1,0:T(8,128)}, bf16[512,3072]{1,0:T(8,128)(2,1)}, bf16[512,3072]{1,0:T(8,128)(2,1)}, f32[8,512]{1,0:T(8,12...) custom-call(s32[8]{0:T(128)} %pad_add_fusion.refs_0_, bf16[1024,7168]{1,0:T(8,128)(2,1)} %all-gather.3.cloned.1.call-done.refs_1_, ...), custom_call_target="tpu_custom_call" | custom-call | flops 10000000000 | bytes 10000000 | tf_op jit(solution)/shard_map/middle/pallas_call | solution.py:626
  152.2 5.6 %collective-permute-done.1 = bf16[512,3072]{1,0:T(8,128)(2,1)S(1)} collective-permute-done((bf16[512,3072]{1,0:T(8,128)(2,1)}, bf16[512,3072]{1,0:T(8,128)(2,1)S(1)}, u32[]{:S(2)}, u32[]{:S(2)}) %collective-permute-start.1) | collective-permute-done | bytes 3145760 | tf_op jit(solution)/shard_map/ppermute | solution.py:722
  157.8 4.7 %add_convert_fusion.refs_28_ = bf16[512,3072]{1,0:T(8,128)(2,1)} fusion(bf16[512,3072]{1,0:T(8,128)(2,1)S(1)} %collective-permute-done.1, bf16[512,3072]{1,0:T(8,128)(2,1)} %get-tuple-element.108), kind=kLoop, calls=%fused_computation | loop fusion | flops 6291456 | bytes 9437184 | tf_op jit(solution)/shard_map/convert_element_type | solution.py:726
  162.6 19.3 %last.1 = (f32[512,512]{1,0:T(8,128)}, f32[512,512]{1,0:T(8,128)}, bf16[512,2176]{1,0:T(8,128)(2,1)}, bf16[512,2176]{1,0:T(8,128)(2,1)}) custom-call(s32[8]{0:T(128)} %pad_add_fusion.refs_0_, bf16[1024,7168]{1,0:T(8,128)(2,1)} %all-gather.3.cloned.1.call-done.refs_1_, f32[32,512]{1,0:T(8,128)} %get-tuple-element.64.refs_2_, ...), custom_call_target="tpu_custom_call" | custom-call | flops 10000000000 | bytes 10000000 | tf_op jit(solution)/shard_map/last/pallas_call | solution.py:626
  182.4 4.2 %collective-permute-done.2 = bf16[512,2176]{1,0:T(8,128)(2,1)S(1)} collective-permute-done((bf16[512,2176]{1,0:T(8,128)(2,1)}, bf16[512,2176]{1,0:T(8,128)(2,1)S(1)}, u32[]{:S(2)}, u32[]{:S(2)}) %collective-permute-start.2) | collective-permute-done | bytes 2228256 | tf_op jit(solution)/shard_map/ppermute | solution.py:722
  186.6 3.5 %add_convert_fusion.1 = bf16[512,2176]{1,0:T(8,128)(2,1)} fusion(bf16[512,2176]{1,0:T(8,128)(2,1)S(1)} %collective-permute-done.2, bf16[512,2176]{1,0:T(8,128)(2,1)} %get-tuple-element.112), kind=kLoop, calls=%fused_computation.2 | loop fusion | flops 4456448 | bytes 6684672 | tf_op jit(solution)/shard_map/convert_element_type | solution.py:726
  190.2 6.7 %all-to-all-start = ((bf16[16,32,2176]{2,1,0:T(8,128)(2,1)}), bf16[16,32,2176]{2,1,0:T(8,128)(2,1)S(1)}, u32[]{:S(2)}, u32[]{:S(2)}) async-start(bf16[16,32,2176]{2,1,0:T(8,128)(2,1)} %bitcast.102), calls=%async_computation.2 | async-start | bytes 4456448 | tf_op jit(solution)/shard_map/all_to_all | solution.py:735
  196.9 30.7 %all-to-all-done = bf16[16,32,2176]{2,1,0:T(8,128)(2,1)S(1)} async-done(((bf16[16,32,2176]{2,1,0:T(8,128)(2,1)}), bf16[16,32,2176]{2,1,0:T(8,128)(2,1)S(1)}, u32[]{:S(2)}, u32[]{:S(2)}) %all-to-all-start) | async-done | bytes 2228256 | tf_op jit(solution)/shard_map/all_to_all | solution.py:735
  227.9 2.3 maximum_bitcast_fusion
  230.2 4.7 %all-to-all-start.1 = ((bf16[16,8,5120]{2,1,0:T(8,128)(2,1)}), bf16[16,8,5120]{2,1,0:T(8,128)(2,1)S(1)}, u32[]{:S(2)}, u32[]{:S(2)}) async-start(bf16[16,8,5120]{2,1,0:T(8,128)(2,1)} %maximum_bitcast_fusion), calls=%async_computation.3 | async-start | bytes 2621440 | tf_op jit(solution)/shard_map/all_to_all | solution.py:735
  235.1 1.7 collective-permute-start.4
  236.7 1.6 collective-permute-start.5
  238.3 0.7 collective-permute-done.3
  240.4 0.7 copy.117
  242.5 10.1 %all-to-all-done.1 = bf16[16,8,5120]{2,1,0:T(8,128)(2,1)S(1)} async-done(((bf16[16,8,5120]{2,1,0:T(8,128)(2,1)}), bf16[16,8,5120]{2,1,0:T(8,128)(2,1)S(1)}, u32[]{:S(2)}, u32[]{:S(2)}) %all-to-all-start.1) | async-done | bytes 1310752 | tf_op jit(solution)/shard_map/all_to_all | solution.py:735
  253.7 3.8 %collective-permute-start.6 = (f32[4,10,512]{2,0,1:T(4,128)S(1)}, f32[4,10,512]{2,0,1:T(4,128)S(1)}, u32[]{:S(2)}, u32[]{:S(2)}) collective-permute-start(f32[4,10,512]{2,0,1:T(4,128)S(1)} %bitcast.114), channel_id=1, source_target_pairs={{0,1},{1,0},{2,3},{3,2},{4,5},{5,4},{6,7},{7,6},{8,9},{9,8},{10,11... | collective-permute-start | bytes 245768 | tf_op jit(solution)/shard_map/ppermute | solution.py:722
  258.6 0.7 reshape.153
  (67 shorter events, 10.2 us)
Async XLA Ops:
  7.2 86.1 %all-gather.3.cloned.1.call-start = ((), (), s32[]{:S(2)}) async-start(), calls=%async_computation.4 | async-start | bytes 14794752 | tf_op jit(solution)/shard_map/all_gather | solution.py:753
  13.5 149.1 %reduce-scatter.3.cloned.1.call-start = ((), (), s32[]{:S(2)}) async-start(), calls=%async_computation.5 | async-start | bytes 2621440 | tf_op jit(solution)/shard_map/reduce_scatter | solution.py:730
  125.5 4.5 %collective-permute-start = (bf16[512,2048]{1,0:T(8,128)(2,1)}, bf16[512,2048]{1,0:T(8,128)(2,1)S(1)}, u32[]{:S(2)}, u32[]{:S(2)}) collective-permute-start(bf16[512,2048]{1,0:T(8,128)(2,1)} %get-tuple-element.84), channel_id=1, source_target_pairs={{0,1},{1,0},{2,3},{3,2},{4,5},{5,4},{6,7},{7,6},{8,9},{9,8},{10,11... | collective-permute-start | bytes 6291464 | tf_op jit(solution)/shard_map/ppermute | solution.py:722
  133.6 94.3 %reduce-scatter.5.cloned.1.call-start = ((), (), s32[]{:S(2)}) async-start(), calls=%async_computation.6 | async-start | bytes 3932160 | tf_op jit(solution)/shard_map/reduce_scatter | solution.py:730
  151.7 6.2 %collective-permute-start.1 = (bf16[512,3072]{1,0:T(8,128)(2,1)}, bf16[512,3072]{1,0:T(8,128)(2,1)S(1)}, u32[]{:S(2)}, u32[]{:S(2)}) collective-permute-start(bf16[512,3072]{1,0:T(8,128)(2,1)} %get-tuple-element.109), channel_id=1, source_target_pairs={{0,1},{1,0},{2,3},{3,2},{4,5},{5,4},{6,7},{7,6},{8,9},{9,8},{10,11... | collective-permute-start | bytes 9437192 | tf_op jit(solution)/shard_map/ppermute | solution.py:722
  181.9 4.7 %collective-permute-start.2 = (bf16[512,2176]{1,0:T(8,128)(2,1)}, bf16[512,2176]{1,0:T(8,128)(2,1)S(1)}, u32[]{:S(2)}, u32[]{:S(2)}) collective-permute-start(bf16[512,2176]{1,0:T(8,128)(2,1)} %get-tuple-element.113), channel_id=1, source_target_pairs={{0,1},{1,0},{2,3},{3,2},{4,5},{5,4},{6,7},{7,6},{8,9},{9,8},{10,11... | collective-permute-start | bytes 6684680 | tf_op jit(solution)/shard_map/ppermute | solution.py:722
  190.2 37.4 %all-to-all-start = ((bf16[16,32,2176]{2,1,0:T(8,128)(2,1)}), bf16[16,32,2176]{2,1,0:T(8,128)(2,1)S(1)}, u32[]{:S(2)}, u32[]{:S(2)}) async-start(bf16[16,32,2176]{2,1,0:T(8,128)(2,1)} %bitcast.102), calls=%async_computation.2 | async-start | bytes 4456448 | tf_op jit(solution)/shard_map/all_to_all | solution.py:735
  196.8 31.1 %copy-start = (bf16[128,2048]{1,0:T(8,128)(2,1)S(1)}, bf16[128,2048]{1,0:T(8,128)(2,1)}, u32[]{:S(2)}) copy-start(bf16[128,2048]{1,0:T(8,128)(2,1)} %reduce-scatter.3.cloned.1.call-done.refs_29_) | copy-start | bytes 1572868
  230.2 22.3 %all-to-all-start.1 = ((bf16[16,8,5120]{2,1,0:T(8,128)(2,1)}), bf16[16,8,5120]{2,1,0:T(8,128)(2,1)S(1)}, u32[]{:S(2)}, u32[]{:S(2)}) async-start(bf16[16,8,5120]{2,1,0:T(8,128)(2,1)} %maximum_bitcast_fusion), calls=%async_computation.3 | async-start | bytes 2621440 | tf_op jit(solution)/shard_map/all_to_all | solution.py:735
  235.0 4.1 %collective-permute-start.3 = (bf16[8,2176]{1,0:T(8,128)(2,1)S(1)}, bf16[8,2176]{1,0:T(8,128)(2,1)S(1)}, u32[]{:S(2)}, u32[]{:S(2)}) collective-permute-start(bf16[8,2176]{1,0:T(8,128)(2,1)S(1)} %get-tuple-element.176), channel_id=1, source_target_pairs={{0,32},{32,64},{64,96},{96,0},{1,33},{33,65},{65,97},{97,1},{2,34}... | collective-permute-start | bytes 104456 | tf_op jit(solution)/shard_map/ppermute | solution.py:745
  235.1 4.4 %collective-permute-start.4 = (bf16[8,2176]{1,0:T(8,128)(2,1)S(1)}, bf16[8,2176]{1,0:T(8,128)(2,1)S(1)}, u32[]{:S(2)}, u32[]{:S(2)}) collective-permute-start(bf16[8,2176]{1,0:T(8,128)(2,1)S(1)} %get-tuple-element.178), channel_id=1, source_target_pairs={{0,64},{32,96},{64,0},{96,32},{1,65},{33,97},{65,1},{97,33},{2,66}... | collective-permute-start | bytes 104456 | tf_op jit(solution)/shard_map/ppermute | solution.py:745
  236.7 3.3 %collective-permute-start.5 = (bf16[8,2176]{1,0:T(8,128)(2,1)S(1)}, bf16[8,2176]{1,0:T(8,128)(2,1)S(1)}, u32[]{:S(2)}, u32[]{:S(2)}) collective-permute-start(bf16[8,2176]{1,0:T(8,128)(2,1)S(1)} %get-tuple-element.177), channel_id=1, source_target_pairs={{0,96},{32,0},{64,32},{96,64},{1,97},{33,1},{65,33},{97,65},{2,98}... | collective-permute-start | bytes 104456 | tf_op jit(solution)/shard_map/ppermute | solution.py:745
  253.7 4.7 %collective-permute-start.6 = (f32[4,10,512]{2,0,1:T(4,128)S(1)}, f32[4,10,512]{2,0,1:T(4,128)S(1)}, u32[]{:S(2)}, u32[]{:S(2)}) collective-permute-start(f32[4,10,512]{2,0,1:T(4,128)S(1)} %bitcast.114), channel_id=1, source_target_pairs={{0,1},{1,0},{2,3},{3,2},{4,5},{5,4},{6,7},{7,6},{8,9},{9,8},{10,11... | collective-permute-start | bytes 245768 | tf_op jit(solution)/shard_map/ppermute | solution.py:722
Sparse Core Ops, SparseCore 0:
  13.6 79.6 all-gather.2
  133.8 28.7 reduce-scatter.2
  165.1 37.9 reduce-scatter.4
where the time goes:
time: 272 us; the launch traced here: 267 us
  waiting for transfers between devices  96.3 us (35%)
  Pallas kernels  71.1 us (26%)
  blocking collectives  36.3 us (13%)
  starting transfers between devices  20.2 us (7%)
  other arithmetic  17.7 us (7%)
  between operations  14.4 us (5%)
  local copies, waits for them, and re-layouts  11.4 us (4%)
    pallas_call x4, Pallas kernels, call(): pl.pallas_call(body, name=name, in_specs=[spec(s) for _, s in inputs], ou...  71.1 us
    all_to_all x2, waiting for transfers between devices, plane_sum(): whole = lax.all_to_all(whole, ('y', 'z'), 0, 0, tiled=True)  40.7 us
    all_gather x1, waiting for transfers between devices, per_device(): gathered = lax.all_gather(shard, AXES, axis=0, tiled=True)  39.5 us
    all_gather x1, blocking collectives, per_device(): vec, bin_vec = run_vectors(lax.all_gather(line, AXES, axis=0, tiled=True))  33.3 us
    ppermute x4, waiting for transfers between devices, swap(): return lax.ppermute(a, 'c', [(0, 1), (1, 0)])  14.3 us
    convert_element_type x3, other arithmetic, pair_sum(): return (mine.astype(F32) + swap(theirs).astype(F32)).astype(BF)  11.9 us
    all_to_all x2, starting transfers between devices, plane_sum(): whole = lax.all_to_all(whole, ('y', 'z'), 0, 0, tiled=True)  11.4 us
  transfers between devices with their start and end apart: 12, of which 10 were waited for; matrix products, arithmetic and copies ran while one was open for 6% of the time, Pallas kernels for 15%

commit v1 on v0

--- a/solution.py
+++ b/solution.py
@@ -272,6 +272,10 @@
     return part.reshape(4, 16, 8, wide).transpose(1, 0, 2, 3).reshape(512, wide)
 
 
+def as_is(part):
+    return part
+
+
 def attn_weight_grads(h_ref, m_ref, o_ref, da_ref, dq_ref, dk_ref, dv_ref, g, turned, base, order):
     def product(side, at, right):
         for n in range(2):
@@ -517,42 +521,52 @@
 
 
 def middle_kernel(scalars, gathered, vec, grad_h, *refs):
-    far_attn, far_ffn = refs[:10], refs[10:15]
-    d1_h, denc_h, mine, theirs, attn_vec, ffn_vec, bin_grad = refs[15:22]
-    near_attn, near_ffn = refs[22:32], refs[32:37]
-    grad, d1, denc, stage, w, w_in, w_out, da, d_o, dq, dk, dv, g, turned, sems = refs[37:]
+    far_cross, far_self, far_ffn = refs[:10], refs[10:19], refs[19:24]
+    dtgt_h, denc_h, mine, theirs, cross_vec, self_vec, ffn_vec, bin_grad = refs[24:32]
+    near_cross, near_self, near_ffn = refs[32:42], refs[42:51], refs[51:56]
+    grad, d1, dtgt, denc, stage, w, w_in, w_out, da, d_o, dq, dk, dv, g, turned, sems = refs[56:]
     moves = Moves(sems)
+    core = scalars[4]
+    temps = (da, d_o, dq, dk, dv, turned)
     grad_in = moves.start(grad_h, grad)
-    pairs = [fetch_pair(moves, gathered, stage, 4 + n, n) for n in range(2)]
-    copies = load_attn(moves, far_attn, near_attn)
-    xh1, inv1, slope, act, enc = near_ffn
-    ffn_in = []
-
-    def arrived():
-        pairs.extend([fetch_pair(moves, gathered, stage, 6 + n, 2 + n) for n in range(4)])
+    cross_pairs = [fetch_pair(moves, gathered, stage, 4 + n, n) for n in range(2)]
+    cross_copies = load_attn(moves, far_cross, near_cross)
+    self_pairs, self_copies, ffn_pairs, ffn_in = [], [], [None, None], []
+
+    def then_self():
+        self_pairs.extend([fetch_pair(moves, gathered, stage, 2 + n, 6 + n) for n in range(2)])
+        self_copies.extend(load_attn(moves, far_self, near_self))
+
+    def then_ffn():
+        ffn_pairs.extend([fetch_pair(moves, gathered, stage, 6 + n, 2 + n) for n in range(4)])
         ffn_in.extend([moves.start(a, b) for a, b in zip(far_ffn, near_ffn)])
 
     bin_grad[...] = jnp.zeros_like(bin_grad)
     grad_in.wait()
     attn_back(
-        grad, near_attn, lambda: prep_attn(stage, 0, pairs, w), w, vec[12:13, :],
-        (da, d_o, dq, dk, dv, turned), d1, grad, g, 0, attn_vec, copies, arrived, lambda part: part,
-    )
-    core = scalars[4]
+        grad, near_cross, lambda: prep_attn(stage, 0, cross_pairs, w), w, vec[12:13, :], temps,
+        d1, grad, g, 0, cross_vec, cross_copies, then_self, as_is,
+    )
     send_gradients(moves, g, core, mine, theirs, 0, 1024)
-    moves.send(d1, d1_h)
+    attn_back(
+        d1, near_self, lambda: prep_attn(stage, 6, [None] * 6 + self_pairs, w), w, vec[11:12, :],
+        temps, dtgt, None, g, 1024, self_vec, self_copies, then_ffn, as_is,
+    )
+    send_gradients(moves, g, core, mine, theirs, 1024, 1024)
+    moves.send(dtgt, dtgt_h)
     for copy in ffn_in:
         copy.wait()
+    xh1, inv1, slope, act, enc = near_ffn
     norm_rows(ffn_vec, grad, xh1, inv1, vec[10:11, :], da, grad)
-    prep_ffn(stage, 2, [None, None] + pairs[2:], w_in, w_out)
+    prep_ffn(stage, 2, ffn_pairs, w_in, w_out)
     ffn_backward(grad, da, w_in, w_out, slope, slope, bin_grad, denc)
     moves.send(denc, denc_h)
 
     def inner_done():
-        send_gradients(moves, g, core, mine, theirs, 1024, 1024)
-
-    ffn_weight_grads(enc, slope, act, da, g, turned, 1024, inner_done)
-    send_gradients(moves, g, core, mine, theirs, 2048, 1024)
+        send_gradients(moves, g, core, mine, theirs, 2048, 1024)
+
+    ffn_weight_grads(enc, slope, act, da, g, turned, 2048, inner_done)
+    send_gradients(moves, g, core, mine, theirs, 3072, 1024)
     moves.finish()
 
 
@@ -578,37 +592,21 @@
         g[side, :, at : at + 128] = block
 
 
-def last_kernel(scalars, gathered, vec, a2_vec, f0_vec, f1_vec, f0_bin, f1_bin, *refs):
-    far_data = [refs[10 * i : 10 * i + 10] for i in range(2)]
-    dx_h, (mine, theirs) = refs[20:22], refs[22:24]
-    near_data = [refs[24 + 10 * i : 34 + 10 * i] for i in range(2)]
-    dx, vec_grad = refs[44:46], refs[46:48]
-    stage, w, da, d_o, dq, dk, dv, g, turned, sems = refs[48:]
+def last_kernel(scalars, gathered, vec, a1_vec, a2_vec, f0_vec, f1_vec, f0_bin, f1_bin, *refs):
+    far_data, (dx_h, mine, theirs), near_data = refs[:10], refs[10:13], refs[13:23]
+    dx, vec_grad, stage, w, da, d_o, dq, dk, dv, g, turned, sems = refs[23:]
     moves = Moves(sems)
-    grads, pairs, copies = [], [], []
-    core = scalars[4]
-
-    def start():
-        i = len(grads)
-        if i < 2:
-            grads.append(moves.start(far_data[i][0], near_data[i][0]))
-            slots = range(2 * i, 2 * i + 2)
-            pairs.extend([fetch_pair(moves, gathered, stage, n, n) for n in slots])
-            copies.append(load_attn(moves, far_data[i][1:], near_data[i][1:]))
-
-    start()
-    for i in range(2):
-        norm = 9 + ATTN_NORMS[i]
-        grads[i].wait()
-        attn_back(
-            near_data[i][0], near_data[i][1:], lambda: prep_attn(stage, 2 * i, pairs, w), w,
-            vec[norm : norm + 1, :], (da, d_o, dq, dk, dv, turned), dx[i], None, g, 1024 * i,
-            vec_grad[i], copies[i], start, planes_first,
-        )
-        if i == 1:
-            write_vectors((*vec_grad, a2_vec), (f0_vec, f1_vec), (f0_bin, f1_bin), g, 2048)
-        send_gradients(moves, g, core, mine, theirs, 1024 * i, 1024 + 128 * i)
-        moves.send(dx[i], dx_h[i])
+    grad_in = moves.start(far_data[0], near_data[0])
+    pairs = [fetch_pair(moves, gathered, stage, n, n) for n in range(2)]
+    copies = load_attn(moves, far_data[1:], near_data[1:])
+    grad_in.wait()
+    attn_back(
+        near_data[0], near_data[1:], lambda: prep_attn(stage, 0, pairs, w), w, vec[9:10, :],
+        (da, d_o, dq, dk, dv, turned), dx, None, g, 0, vec_grad, copies, lambda: None, planes_first,
+    )
+    write_vectors((vec_grad, a1_vec, a2_vec), (f0_vec, f1_vec), (f0_bin, f1_bin), g, 1024)
+    send_gradients(moves, g, scalars[4], mine, theirs, 0, 1152)
+    moves.send(dx, dx_h)
     moves.finish()
 
 
@@ -683,25 +681,26 @@
     return [xh, inv, r, o, q, v, k, e, *rows]
 
 
-def run_middle(scalars, gathered, vec, grad, attn, ffn, after=()):
-    kinds = ATTN_DATA + [ROW] + [ROW, INV, WIDE, WIDE, ROW]
-    inputs = [(scalars, S), (gathered, H), (vec, V)] + [(a, H) for a in (grad, *attn, *ffn)]
-    outs = far([LINE, LINE]) + [((D, 3072), BF, H)] * 2 + [VEC, VEC, BIN]
-    scratch = near(kinds) + near([LINE] * 3) + [
-        V((6, 1024, 512), BF), V((4, 512, 512), BF), V((D, FF), BF), V((FF, D), BF),
-        *near([ROW] * 5), V((2, D, 3072), BF), V((D, ALL), BF), pltpu.SemaphoreType.DMA((40,)),
+def run_middle(scalars, gathered, vec, grad, cross, own, ffn, after=()):
+    kinds = ATTN_DATA + [ROW] + ATTN_DATA + [ROW, INV, WIDE, WIDE, ROW]
+    inputs = [(scalars, S), (gathered, H), (vec, V)]
+    inputs += [(a, H) for a in (grad, *cross, *own, *ffn)]
+    outs = far([LINE, LINE]) + [((D, 4096), BF, H)] * 2 + [VEC, VEC, VEC, BIN]
+    scratch = near(kinds) + near([LINE] * 4) + [
+        V((8, 1024, 512), BF), V((4, 512, 512), BF), V((D, FF), BF), V((FF, D), BF),
+        *near([ROW] * 5), V((2, D, 4096), BF), V((D, ALL), BF), pltpu.SemaphoreType.DMA((56,)),
     ]
     return call(middle_kernel, "middle", inputs, outs, scratch, after)
 
 
 def run_last(scalars, gathered, vec, sums, data, after=()):
-    kinds = ([LINE] + ATTN_DATA) * 2
+    kinds = [LINE] + ATTN_DATA
     inputs = [(scalars, S), (gathered, H), (vec, V)]
     inputs += [(a, V) for a in sums] + [(a, H) for a in data]
-    outs = far([LINE, LINE]) + [((D, 2176), BF, H)] * 2
-    scratch = near(kinds) + near([LINE] * 2) + [V((8, D), F32), V((8, D), F32)] + [
-        V((4, 1024, 512), BF), V((4, 512, 512), BF), *near([ROW] * 5), V((2, D, 2176), BF),
-        V((D, ALL), BF), pltpu.SemaphoreType.DMA((40,)),
+    outs = far([LINE]) + [((D, 1152), BF, H)] * 2
+    scratch = near(kinds) + near([LINE]) + [
+        V((8, D), F32), V((2, 1024, 512), BF), V((4, 512, 512), BF), *near([ROW] * 5),
+        V((2, D, 1152), BF), V((D, ALL), BF), pltpu.SemaphoreType.DMA((24,)),
     ]
     return call(last_kernel, "last", inputs, outs, scratch, after)
 
@@ -763,27 +762,29 @@
     enc, mem, first, act0, slope0, f1_mine, f1_theirs, f1_vec, f1_bin = outs[28:]
     f1 = pair_sum(f1_mine, f1_theirs)
     f1_x = ring_sum(f1)
-    d1, d_enc, mid_mine, mid_theirs, a2_vec, f0_vec, f0_bin = run_middle(
+    d_tgt, d_enc, mid_mine, mid_theirs, a2_vec, a1_vec, f0_vec, f0_bin = run_middle(
         scalars, gathered, vec, grad, attn_data(xh[3], inv[3], heads[2], first, mem),
-        [xh[1], inv[1], slope0, act0, enc], (f1,),
-    )
+        attn_data(xh[2], inv[2], heads[1], tgt), [xh[1], inv[1], slope0, act0, enc], (f1,),
+    )
+    f1_x, mid_mine = lax.optimization_barrier((f1_x, mid_mine))
     mid = pair_sum(mid_mine, mid_theirs)
     mid_x = ring_sum(mid)
-    data = [d_enc, *attn_data(xh[0], inv[0], heads[0], src)]
-    data += [d1, *attn_data(xh[2], inv[2], heads[1], tgt)]
-    d_src, d_tgt, end_mine, end_theirs = run_last(
-        scalars, gathered, vec, (a2_vec, f0_vec, f1_vec, f0_bin, f1_bin), data, (mid, f1_x)
+    d_src, end_mine, end_theirs = run_last(
+        scalars, gathered, vec, (a1_vec, a2_vec, f0_vec, f1_vec, f0_bin, f1_bin),
+        [d_enc, *attn_data(xh[0], inv[0], heads[0], src)], (mid,),
     )
     end = plane_sum(pair_sum(end_mine, end_theirs))
-    mid_x, end = lax.optimization_barrier((mid_x, end))
+    f1_x, end = lax.optimization_barrier((f1_x, end))
+    sum_f1 = plane_sum(f1_x)
+    mid_x, sum_f1 = lax.optimization_barrier((mid_x, sum_f1))
+    sum_mid = plane_sum(mid_x)
     sum_end = line_sum(end)
-    sum_rest = plane_sum(jnp.concatenate([mid_x, f1_x], axis=1))
-
-    cut = sum_end[:, 2048:]
+
+    cut = sum_end[:, 1024:]
     vecs = cut[:, :24].reshape(8, 3, 2, 4).transpose(1, 0, 2, 3).reshape(24, 2, 4)
     vecs = lax.dynamic_index_in_dim(vecs, c, 1, False)
     g_bin = lax.dynamic_index_in_dim(cut[:2, 32:64].reshape(2, 2, 16), c, 1, False)
-    whole = jnp.concatenate([sum_end[:, :2048], sum_rest], axis=1)
+    whole = jnp.concatenate([sum_end[:, :1024], sum_mid[:, 1024:2048], sum_mid[:, :1024], sum_mid[:, 2048:], sum_f1], axis=1)
     attn = whole[:, :3072].reshape(2, 4, 6, 512)
     wide = whole[:, 3072:].reshape(8, 2, 4, 512)
     rows = jnp.concatenate([attn, wide[:, :, :2].reshape(2, 4, 4, 512)], axis=2)

time: 272 us -> 265 us (0.974)
  waiting for transfers between devices: 96.3 us -> 71.4 us
  blocking collectives: 36.3 us -> 59.6 us
  starting transfers between devices: 20.2 us -> 17.2 us
    all_to_all x2, waiting for transfers between devices: 40.7 us -> 15.2 us  [plane_sum(): whole = lax.all_to_all(whole, ('y', 'z'), 0, 0, tiled=True)]
    all_to_all x0 -> x1, blocking collectives: none -> 23.3 us  [plane_sum(): whole = lax.all_to_all(whole, ('y', 'z'), 0, 0, tiled=True)]
    all_to_all x2, starting transfers between devices: 11.4 us -> 7.91 us  [plane_sum(): whole = lax.all_to_all(whole, ('y', 'z'), 0, 0, tiled=True)]
    reduce_scatter x2, waiting for transfers between devices: 0.04 us -> 3.28 us  [ring_sum(): return lax.psum_scatter(whole, 'x', scatter_dimension=0, tiled=True)]
    ppermute x4, waiting for transfers between devices: 14.3 us -> 11.3 us  [swap(): return lax.ppermute(a, 'c', [(0, 1), (1, 0)])]
  transfers between devices with their start and end apart: 12 -> 12, of which waited for: 10 -> 11; matrix products, arithmetic and copies ran while one was open for 6% -> 4% of each run, Pallas kernels for 15% -> 15%
where the time goes in v1:
time: 265 us; the launch traced here: 260 us
  waiting for transfers between devices  71.4 us (27%)
  Pallas kernels  70.7 us (27%)
  blocking collectives  59.6 us (22%)
  starting transfers between devices  17.2 us (6%)
  other arithmetic  15.2 us (6%)
  between operations  14.3 us (5%)
  local copies, waits for them, and re-layouts  11.4 us (4%)
    pallas_call x4, Pallas kernels, call(): pl.pallas_call(body, name=name, in_specs=[spec(s) for _, s in inputs], ou...  70.7 us
    all_gather x1, waiting for transfers between devices, per_device(): gathered = lax.all_gather(shard, AXES, axis=0, tiled=True)  40.1 us
    all_gather x1, blocking collectives, per_device(): vec, bin_vec = run_vectors(lax.all_gather(line, AXES, axis=0, tiled=True))  33.3 us
    all_to_all x1, blocking collectives, plane_sum(): whole = lax.all_to_all(whole, ('y', 'z'), 0, 0, tiled=True)  23.3 us
    all_to_all x2, waiting for transfers between devices, plane_sum(): whole = lax.all_to_all(whole, ('y', 'z'), 0, 0, tiled=True)  15.2 us
    convert_element_type x3, other arithmetic, pair_sum(): return (mine.astype(F32) + swap(theirs).astype(F32)).astype(BF)  12.5 us
    ppermute x4, waiting for transfers between devices, swap(): return lax.ppermute(a, 'c', [(0, 1), (1, 0)])  11.3 us
    all_to_all x2, starting transfers between devices, plane_sum(): whole = lax.all_to_all(whole, ('y', 'z'), 0, 0, tiled=True)  7.91 us
  transfers between devices with their start and end apart: 12, of which 11 were waited for; matrix products, arithmetic and copies ran while one was open for 4% of the time, Pallas kernels for 15%

profile of v1, /device:TPU:1, one launch (start us, length us, event | category | flops | bytes accessed | tf_op | source)
XLA Modules:
  0.0 259.9 jit_solution(15275182591451498772)
XLA Ops:
  7.2 0.8 fusion.8
  8.1 0.8 pad_maximum_fusion.4
  9.0 3.0 %all_gather.9 = bf16[20,8,512]{2,0,1:T(8,128)(2,1)S(1)} all-gather(bf16[20,4,512]{2,0,1:T(8,128)(2,1)S(1)} %copy.100), channel_id=1, replica_groups=mesh['x'=4,'y'=4,'z'=4,'c'=2] {'c'}, dimensions={1}, use_global_device_ids=true | all-gather | bytes 245760 | tf_op jit(solution)/shard_map/all_gather | solution.py:711
  12.1 0.7 slice_bitcast_fusion.6
  13.6 0.7 reshape.163
  14.4 0.7 reshape.137
  15.2 0.8 copy.103
  16.0 0.8 concatenate.33
  16.9 33.3 %all-gather = bf16[128,1,128]{2,1,0:T(2,128)(2,1)S(1)} all-gather(bf16[1,1,128]{2,1,0:T(2,128)(2,1)S(1)} %reshape.160), channel_id=1, replica_groups=mesh['x'=4,'y'=4,'z'=4,'c'=2] {'x','y','z','c'}, dimensions={0}, use_global_device_ids=true | all-gather | bytes 33024 | tf_op jit(solution)/shard_map/all_gather | solution.py:753
  51.4 1.9 vectors.1
  53.2 40.1 %all-gather.3.cloned.1.call-done.refs_1_ = bf16[1024,7168]{1,0:T(8,128)(2,1)} async-done(((bf16[8,7168]{1,0:T(8,128)(2,1)}), bf16[1024,7168]{1,0:T(8,128)(2,1)}) %all-gather.3.cloned.1.call-update) | async-done | bytes 14680080 | tf_op jit(solution)/shard_map/all_gather | solution.py:752
  93.3 32.0 %forward.1 = (bf16[512,512]{1,0:T(8,128)(2,1)}, f32[512,512]{1,0:T(8,128)}, bf16[512,512]{1,0:T(8,128)(2,1)}, bf16[512,512]{1,0:T(8,128)(2,1)}, bf16[512,512]{1,...) custom-call(s32[8]{0:T(128)} %pad_add_fusion.refs_0_, ...), custom_call_target="tpu_custom_call" | custom-call | flops 10000000000 | bytes 10000000 | tf_op jit(solution)/shard_map/forward/pallas_call | solution.py:624
  125.7 4.1 %collective-permute-done = bf16[512,2048]{1,0:T(8,128)(2,1)S(1)} collective-permute-done((bf16[512,2048]{1,0:T(8,128)(2,1)}, bf16[512,2048]{1,0:T(8,128)(2,1)S(1)}, u32[]{:S(2)}, u32[]{:S(2)}) %collective-permute-start) | collective-permute-done | bytes 2097184 | tf_op jit(solution)/shard_map/ppermute | solution.py:721
  129.8 3.7 %add_convert_fusion.1.refs_28_ = bf16[512,2048]{1,0:T(8,128)(2,1)} fusion(bf16[512,2048]{1,0:T(8,128)(2,1)S(1)} %collective-permute-done, bf16[512,2048]{1,0:T(8,128)(2,1)} %get-tuple-element.95), kind=kLoop, calls=%fused_computation.1 | loop fusion | flops 4194304 | bytes 6291456 | tf_op jit(solution)/shard_map/convert_element_type | solution.py:725
  134.0 24.9 %middle.1 = (f32[512,512]{1,0:T(8,128)}, f32[512,512]{1,0:T(8,128)}, bf16[512,4096]{1,0:T(8,128)(2,1)}, bf16[512,4096]{1,0:T(8,128)(2,1)}, f32[8,512]{1,0:T(8,12...) custom-call(s32[8]{0:T(128)} %pad_add_fusion.refs_0_, ...), custom_call_target="tpu_custom_call" | custom-call | flops 10000000000 | bytes 10000000 | tf_op jit(solution)/shard_map/middle/pallas_call | solution.py:624
  159.2 3.3 %reduce-scatter.3.cloned.1.call-done = bf16[128,2048]{1,0:T(8,128)(2,1)} async-done(((bf16[512,2048]{1,0:T(8,128)(2,1)}), bf16[128,2048]{1,0:T(8,128)(2,1)}) %reduce-scatter.3.cloned.1.call-update) | async-done | bytes 524304 | tf_op jit(solution)/shard_map/reduce_scatter | solution.py:729
  162.4 4.0 %collective-permute-done.1 = bf16[512,4096]{1,0:T(8,128)(2,1)} collective-permute-done((bf16[512,4096]{1,0:T(8,128)(2,1)}, bf16[512,4096]{1,0:T(8,128)(2,1)}, u32[]{:S(2)}, u32[]{:S(2)}) %collective-permute-start.1) | collective-permute-done | bytes 4194336 | tf_op jit(solution)/shard_map/ppermute | solution.py:721
  166.4 7.3 %add_convert_fusion.refs_19_ = bf16[512,4096]{1,0:T(8,128)(2,1)} fusion(bf16[512,4096]{1,0:T(8,128)(2,1)} %collective-permute-done.1, bf16[512,4096]{1,0:T(8,128)(2,1)} %get-tuple-element.113), kind=kLoop, calls=%fused_computation | loop fusion | flops 8388608 | bytes 12582912 | tf_op jit(solution)/shard_map/convert_element_type | solution.py:725
  173.7 12.0 %last.1 = (f32[512,512]{1,0:T(8,128)}, bf16[512,1152]{1,0:T(8,128)(2,1)}, bf16[512,1152]{1,0:T(8,128)(2,1)}) custom-call(s32[8]{0:T(128)} %pad_add_fusion.refs_0_, bf16[1024,7168]{1,0:T(8,128)(2,1)} %all-gather.3.cloned.1.call-done.refs_1_, f32[32,512]{1,0:T(8,128)} %get-tuple-element.68.refs_2_, f32[8,512]{1,0:T(8,128)} %get-tuple-element.97.refs_3_, ...), custom_call_target="tpu_custom_call" | custom-call | flops 10000000000 | bytes 10000000 | tf_op jit(solution)/shard_map/last/pallas_call | solution.py:624
  186.1 2.8 %collective-permute-done.2 = bf16[512,1152]{1,0:T(8,128)(2,1)S(1)} collective-permute-done((bf16[512,1152]{1,0:T(8,128)(2,1)}, bf16[512,1152]{1,0:T(8,128)(2,1)S(1)}, u32[]{:S(2)}, u32[]{:S(2)}) %collective-permute-start.2) | collective-permute-done | bytes 1179680 | tf_op jit(solution)/shard_map/ppermute | solution.py:721
  188.9 1.6 add_convert_fusion.2
  190.4 23.3 %all_to_all.15 = bf16[16,32,1152]{2,1,0:T(8,128)(2,1)S(1)} all-to-all(bf16[16,32,1152]{2,1,0:T(8,128)(2,1)S(1)} %bitcast.102), channel_id=1, replica_groups=mesh['x'=4,'y'=4,'z'=4,'c'=2] {'y','z'}, dimensions={0} | all-to-all | bytes 2359296 | tf_op jit(solution)/shard_map/all_to_all | solution.py:734
  213.9 3.6 %all-to-all-start.1 = ((bf16[16,8,2048]{2,1,0:T(8,128)(2,1)}), bf16[16,8,2048]{2,1,0:T(8,128)(2,1)S(1)}, u32[]{:S(2)}, u32[]{:S(2)}) async-start(bf16[16,8,2048]{2,1,0:T(8,128)(2,1)} %bitcast.29), calls=%async_computation.3 | async-start | bytes 1048576 | tf_op jit(solution)/shard_map/all_to_all | solution.py:734
  217.6 8.8 %all-to-all-done.1 = bf16[16,8,2048]{2,1,0:T(8,128)(2,1)S(1)} async-done(((bf16[16,8,2048]{2,1,0:T(8,128)(2,1)}), bf16[16,8,2048]{2,1,0:T(8,128)(2,1)S(1)}, u32[]{:S(2)}, u32[]{:S(2)}) %all-to-all-start.1) | async-done | bytes 524320 | tf_op jit(solution)/shard_map/all_to_all | solution.py:734
  226.6 4.3 %all-to-all-start.2 = ((bf16[16,8,4096]{2,1,0:T(8,128)(2,1)}), bf16[16,8,4096]{2,1,0:T(8,128)(2,1)S(1)}, u32[]{:S(2)}, u32[]{:S(2)}) async-start(bf16[16,8,4096]{2,1,0:T(8,128)(2,1)} %bitcast.103), calls=%async_computation.4 | async-start | bytes 2097152 | tf_op jit(solution)/shard_map/all_to_all | solution.py:734
  231.1 2.5 collective-permute-start.4
  233.6 1.1 collective-permute-start.5
  235.2 1.0 collective-permute-done.5
  236.6 0.7 copy.118
  238.7 6.4 %all-to-all-done.2 = bf16[16,8,4096]{2,1,0:T(8,128)(2,1)S(1)} async-done(((bf16[16,8,4096]{2,1,0:T(8,128)(2,1)}), bf16[16,8,4096]{2,1,0:T(8,128)(2,1)S(1)}, u32[]{:S(2)}, u32[]{:S(2)}) %all-to-all-start.2) | async-done | bytes 1048608 | tf_op jit(solution)/shard_map/all_to_all | solution.py:734
  246.2 3.9 %collective-permute-start.6 = (f32[4,10,512]{2,0,1:T(4,128)S(1)}, f32[4,10,512]{2,0,1:T(4,128)S(1)}, u32[]{:S(2)}, u32[]{:S(2)}) collective-permute-start(f32[4,10,512]{2,0,1:T(4,128)S(1)} %bitcast.115), channel_id=1, source_target_pairs={{0,1},{1,0},{2,3},{3,2},{4,5},{5,4},{6,7},{7,6},{8,9},{9,8},{10,11... | collective-permute-start | bytes 245768 | tf_op jit(solution)/shard_map/ppermute | solution.py:721
  251.2 0.7 reshape.157
  (72 shorter events, 10.2 us)
Async XLA Ops:
  7.2 43.6 %copy-start.1 = (s32[2,1]{0,1:T(1,128)S(1)}, s32[2,1]{0,1:T(1,128)}, u32[]{:S(2)}) copy-start(s32[2,1]{0,1:T(1,128)} %param.16) | copy-start | bytes 28
  7.2 43.6 %copy-start = (s32[2,1]{0,1:T(1,128)S(1)}, s32[2,1]{0,1:T(1,128)}, u32[]{:S(2)}) copy-start(s32[2,1]{0,1:T(1,128)} %param.17) | copy-start | bytes 28
  7.2 86.1 %all-gather.3.cloned.1.call-start = ((), (), s32[]{:S(2)}) async-start(), calls=%async_computation.5 | async-start | bytes 14794752 | tf_op jit(solution)/shard_map/all_gather | solution.py:752
  13.5 148.9 %reduce-scatter.3.cloned.1.call-start = ((), (), s32[]{:S(2)}) async-start(), calls=%async_computation.6 | async-start | bytes 2621440 | tf_op jit(solution)/shard_map/reduce_scatter | solution.py:729
  125.4 4.5 %collective-permute-start = (bf16[512,2048]{1,0:T(8,128)(2,1)}, bf16[512,2048]{1,0:T(8,128)(2,1)S(1)}, u32[]{:S(2)}, u32[]{:S(2)}) collective-permute-start(bf16[512,2048]{1,0:T(8,128)(2,1)} %get-tuple-element.96), channel_id=1, source_target_pairs={{0,1},{1,0},{2,3},{3,2},{4,5},{5,4},{6,7},{7,6},{8,9},{9,8},{10,11... | collective-permute-start | bytes 6291464 | tf_op jit(solution)/shard_map/ppermute | solution.py:721
  133.5 93.0 %reduce-scatter.5.cloned.1.call-start = ((), (), s32[]{:S(2)}) async-start(), calls=%async_computation.7 | async-start | bytes 5242880 | tf_op jit(solution)/shard_map/reduce_scatter | solution.py:729
  158.8 7.6 %collective-permute-start.1 = (bf16[512,4096]{1,0:T(8,128)(2,1)}, bf16[512,4096]{1,0:T(8,128)(2,1)}, u32[]{:S(2)}, u32[]{:S(2)}) collective-permute-start(bf16[512,4096]{1,0:T(8,128)(2,1)} %get-tuple-element.114), channel_id=1, source_target_pairs={{0,1},{1,0},{2,3},{3,2},{4,5},{5,4},{6,7},{7,6},{8,9},{9,8},{10,11... | collective-permute-start | bytes 12582920 | tf_op jit(solution)/shard_map/ppermute | solution.py:721
  185.7 3.1 %collective-permute-start.2 = (bf16[512,1152]{1,0:T(8,128)(2,1)}, bf16[512,1152]{1,0:T(8,128)(2,1)S(1)}, u32[]{:S(2)}, u32[]{:S(2)}) collective-permute-start(bf16[512,1152]{1,0:T(8,128)(2,1)} %get-tuple-element.119), channel_id=1, source_target_pairs={{0,1},{1,0},{2,3},{3,2},{4,5},{5,4},{6,7},{7,6},{8,9},{9,8},{10,11... | collective-permute-start | bytes 3538952 | tf_op jit(solution)/shard_map/ppermute | solution.py:721
  213.9 12.5 %all-to-all-start.1 = ((bf16[16,8,2048]{2,1,0:T(8,128)(2,1)}), bf16[16,8,2048]{2,1,0:T(8,128)(2,1)S(1)}, u32[]{:S(2)}, u32[]{:S(2)}) async-start(bf16[16,8,2048]{2,1,0:T(8,128)(2,1)} %bitcast.29), calls=%async_computation.3 | async-start | bytes 1048576 | tf_op jit(solution)/shard_map/all_to_all | solution.py:734
  226.6 18.5 %all-to-all-start.2 = ((bf16[16,8,4096]{2,1,0:T(8,128)(2,1)}), bf16[16,8,4096]{2,1,0:T(8,128)(2,1)S(1)}, u32[]{:S(2)}, u32[]{:S(2)}) async-start(bf16[16,8,4096]{2,1,0:T(8,128)(2,1)} %bitcast.103), calls=%async_computation.4 | async-start | bytes 2097152 | tf_op jit(solution)/shard_map/all_to_all | solution.py:734
  230.9 3.9 %collective-permute-start.3 = (bf16[8,1152]{1,0:T(8,128)(2,1)S(1)}, bf16[8,1152]{1,0:T(8,128)(2,1)S(1)}, u32[]{:S(2)}, u32[]{:S(2)}) collective-permute-start(bf16[8,1152]{1,0:T(8,128)(2,1)S(1)} %get-tuple-element.188), channel_id=1, source_target_pairs={{0,32},{32,64},{64,96},{96,0},{1,33},{33,65},{65,97},{97,1},{2,34}... | collective-permute-start | bytes 55304 | tf_op jit(solution)/shard_map/ppermute | solution.py:744
  231.1 4.1 %collective-permute-start.4 = (bf16[8,1152]{1,0:T(8,128)(2,1)S(1)}, bf16[8,1152]{1,0:T(8,128)(2,1)S(1)}, u32[]{:S(2)}, u32[]{:S(2)}) collective-permute-start(bf16[8,1152]{1,0:T(8,128)(2,1)S(1)} %get-tuple-element.190), channel_id=1, source_target_pairs={{0,64},{32,96},{64,0},{96,32},{1,65},{33,97},{65,1},{97,33},{2,66}... | collective-permute-start | bytes 55304 | tf_op jit(solution)/shard_map/ppermute | solution.py:744
  233.6 2.6 %collective-permute-start.5 = (bf16[8,1152]{1,0:T(8,128)(2,1)S(1)}, bf16[8,1152]{1,0:T(8,128)(2,1)S(1)}, u32[]{:S(2)}, u32[]{:S(2)}) collective-permute-start(bf16[8,1152]{1,0:T(8,128)(2,1)S(1)} %get-tuple-element.189), channel_id=1, source_target_pairs={{0,96},{32,0},{64,32},{96,64},{1,97},{33,1},{65,33},{97,65},{2,98}... | collective-permute-start | bytes 55304 | tf_op jit(solution)/shard_map/ppermute | solution.py:744
  246.2 4.8 %collective-permute-start.6 = (f32[4,10,512]{2,0,1:T(4,128)S(1)}, f32[4,10,512]{2,0,1:T(4,128)S(1)}, u32[]{:S(2)}, u32[]{:S(2)}) collective-permute-start(f32[4,10,512]{2,0,1:T(4,128)S(1)} %bitcast.115), channel_id=1, source_target_pairs={{0,1},{1,0},{2,3},{3,2},{4,5},{5,4},{6,7},{7,6},{8,9},{9,8},{10,11... | collective-permute-start | bytes 245768 | tf_op jit(solution)/shard_map/ppermute | solution.py:721
Sparse Core Ops, SparseCore 0:
  13.6 79.6 all-gather.2
  133.6 28.7 reduce-scatter.2
  173.8 45.8 reduce-scatter.4

commit v2 on v1

--- a/solution.py
+++ b/solution.py
@@ -221,7 +221,7 @@
     lax.fori_loop(0, PAIRS, pair, 0, unroll=True)
 
 
-def ffn_backward(dr, df, w_in, w_out, slope_ref, du_ref, bin_grad, dx):
+def ffn_hidden_backward(df, w_out, slope_ref, du_ref, bin_grad):
     def hidden(cols):
         du = nt(df[...], w_out[cols, :]) * slope_ref[:, cols].astype(F32)
         bin_grad[0:1, cols] = jnp.sum(du, 0, keepdims=True)
@@ -229,6 +229,8 @@
 
     blocks(256, FF, hidden)
 
+
+def ffn_input_backward(dr, w_in, du_ref, dx):
     def pair(b, carry):
         rows = rows_of(b)
         dx[rows, :] = dr[rows, :] + nt(du_ref[rows, :], w_in[...])
@@ -440,8 +442,7 @@
         from_x32, second, w_in, w_out, bin_vec.at[1:2], vec[20:21, :], act1, slope1, last
     )
     moves.send(dec, dec_h)
-    ffn_backward(x32, df, w_in, w_out, slope1, slope1, bin_grad, grad_d2)
-    moves.send(grad_d2, grad_h)
+    ffn_hidden_backward(df, w_out, slope1, slope1, bin_grad)
     core = scalars[4]
 
     def inner_done():
@@ -449,6 +450,8 @@
 
     ffn_weight_grads(second, slope1, act1, df, g, turned, 0, inner_done)
     send_gradients(moves, g, core, mine, theirs, 1024, 1024)
+    ffn_input_backward(x32, w_in, slope1, grad_d2)
+    moves.send(grad_d2, grad_h)
     moves.finish()
 
 
@@ -559,14 +562,15 @@
     xh1, inv1, slope, act, enc = near_ffn
     norm_rows(ffn_vec, grad, xh1, inv1, vec[10:11, :], da, grad)
     prep_ffn(stage, 2, ffn_pairs, w_in, w_out)
-    ffn_backward(grad, da, w_in, w_out, slope, slope, bin_grad, denc)
-    moves.send(denc, denc_h)
+    ffn_hidden_backward(da, w_out, slope, slope, bin_grad)
 
     def inner_done():
         send_gradients(moves, g, core, mine, theirs, 2048, 1024)
 
     ffn_weight_grads(enc, slope, act, da, g, turned, 2048, inner_done)
     send_gradients(moves, g, core, mine, theirs, 3072, 1024)
+    ffn_input_backward(grad, w_in, slope, denc)
+    moves.send(denc, denc_h)
     moves.finish()
 
 

time: 265 us -> 264 us (level)
  no operation moved by 1% of the time
where the time goes in v2:
time: 264 us; the launch traced here: 259 us
  waiting for transfers between devices  71.5 us (27%)
  Pallas kernels  70.1 us (27%)
  blocking collectives  59.6 us (23%)
  starting transfers between devices  17.1 us (6%)
  other arithmetic  15.2 us (6%)
  between operations  14.3 us (5%)
  local copies, waits for them, and re-layouts  11.4 us (4%)
    pallas_call x4, Pallas kernels, call(): pl.pallas_call(body, name=name, in_specs=[spec(s) for _, s in inputs], ou...  70.1 us
    all_gather x1, waiting for transfers between devices, per_device(): gathered = lax.all_gather(shard, AXES, axis=0, tiled=True)  40.1 us
    all_gather x1, blocking collectives, per_device(): vec, bin_vec = run_vectors(lax.all_gather(line, AXES, axis=0, tiled=True))  33.3 us
    all_to_all x1, blocking collectives, plane_sum(): whole = lax.all_to_all(whole, ('y', 'z'), 0, 0, tiled=True)  23.3 us
    all_to_all x2, waiting for transfers between devices, plane_sum(): whole = lax.all_to_all(whole, ('y', 'z'), 0, 0, tiled=True)  15.2 us
    convert_element_type x3, other arithmetic, pair_sum(): return (mine.astype(F32) + swap(theirs).astype(F32)).astype(BF)  12.5 us
    ppermute x4, waiting for transfers between devices, swap(): return lax.ppermute(a, 'c', [(0, 1), (1, 0)])  11 us
    all_to_all x2, starting transfers between devices, plane_sum(): whole = lax.all_to_all(whole, ('y', 'z'), 0, 0, tiled=True)  7.91 us
  transfers between devices with their start and end apart: 12, of which 11 were waited for; matrix products, arithmetic and copies ran while one was open for 4% of the time, Pallas kernels for 15%

profile of v2, /device:TPU:1, one launch (start us, length us, event | category | flops | bytes accessed | tf_op | source)
XLA Modules:
  0.0 259.3 jit_solution(15159773836842400498)
XLA Ops:
  7.2 0.8 fusion.8
  8.1 0.8 pad_maximum_fusion.4
  9.0 3.0 %all_gather.9 = bf16[20,8,512]{2,0,1:T(8,128)(2,1)S(1)} all-gather(bf16[20,4,512]{2,0,1:T(8,128)(2,1)S(1)} %copy.100), channel_id=1, replica_groups=mesh['x'=4,'y'=4,'z'=4,'c'=2] {'c'}, dimensions={1}, use_global_device_ids=true | all-gather | bytes 245760 | tf_op jit(solution)/shard_map/all_gather | solution.py:715
  12.1 0.7 slice_bitcast_fusion.6
  13.6 0.7 reshape.163
  14.4 0.7 reshape.137
  15.2 0.8 copy.103
  16.0 0.8 concatenate.33
  16.9 33.3 %all-gather = bf16[128,1,128]{2,1,0:T(2,128)(2,1)S(1)} all-gather(bf16[1,1,128]{2,1,0:T(2,128)(2,1)S(1)} %reshape.160), channel_id=1, replica_groups=mesh['x'=4,'y'=4,'z'=4,'c'=2] {'x','y','z','c'}, dimensions={0}, use_global_device_ids=true | all-gather | bytes 33024 | tf_op jit(solution)/shard_map/all_gather | solution.py:757
  51.4 1.9 vectors.1
  53.2 40.1 %all-gather.3.cloned.1.call-done.refs_1_ = bf16[1024,7168]{1,0:T(8,128)(2,1)} async-done(((bf16[8,7168]{1,0:T(8,128)(2,1)}), bf16[1024,7168]{1,0:T(8,128)(2,1)}) %all-gather.3.cloned.1.call-update) | async-done | bytes 14680080 | tf_op jit(solution)/shard_map/all_gather | solution.py:756
  93.3 31.7 %forward.1 = (bf16[512,512]{1,0:T(8,128)(2,1)}, f32[512,512]{1,0:T(8,128)}, bf16[512,512]{1,0:T(8,128)(2,1)}, bf16[512,512]{1,0:T(8,128)(2,1)}, bf16[512,512]{1,...) custom-call(s32[8]{0:T(128)} %pad_add_fusion.refs_0_, ...), custom_call_target="tpu_custom_call" | custom-call | flops 10000000000 | bytes 10000000 | tf_op jit(solution)/shard_map/forward/pallas_call | solution.py:628
  125.3 4.1 %collective-permute-done = bf16[512,2048]{1,0:T(8,128)(2,1)S(1)} collective-permute-done((bf16[512,2048]{1,0:T(8,128)(2,1)}, bf16[512,2048]{1,0:T(8,128)(2,1)S(1)}, u32[]{:S(2)}, u32[]{:S(2)}) %collective-permute-start) | collective-permute-done | bytes 2097184 | tf_op jit(solution)/shard_map/ppermute | solution.py:725
  129.5 3.7 %add_convert_fusion.1.refs_28_ = bf16[512,2048]{1,0:T(8,128)(2,1)} fusion(bf16[512,2048]{1,0:T(8,128)(2,1)S(1)} %collective-permute-done, bf16[512,2048]{1,0:T(8,128)(2,1)} %get-tuple-element.95), kind=kLoop, calls=%fused_computation.1 | loop fusion | flops 4194304 | bytes 6291456 | tf_op jit(solution)/shard_map/convert_element_type | solution.py:729
  133.6 24.6 %middle.1 = (f32[512,512]{1,0:T(8,128)}, f32[512,512]{1,0:T(8,128)}, bf16[512,4096]{1,0:T(8,128)(2,1)}, bf16[512,4096]{1,0:T(8,128)(2,1)}, f32[8,512]{1,0:T(8,12...) custom-call(s32[8]{0:T(128)} %pad_add_fusion.refs_0_, ...), custom_call_target="tpu_custom_call" | custom-call | flops 10000000000 | bytes 10000000 | tf_op jit(solution)/shard_map/middle/pallas_call | solution.py:628
  158.5 3.6 %reduce-scatter.3.cloned.1.call-done = bf16[128,2048]{1,0:T(8,128)(2,1)} async-done(((bf16[512,2048]{1,0:T(8,128)(2,1)}), bf16[128,2048]{1,0:T(8,128)(2,1)}) %reduce-scatter.3.cloned.1.call-update) | async-done | bytes 524304 | tf_op jit(solution)/shard_map/reduce_scatter | solution.py:733
  162.1 3.7 %collective-permute-done.1 = bf16[512,4096]{1,0:T(8,128)(2,1)} collective-permute-done((bf16[512,4096]{1,0:T(8,128)(2,1)}, bf16[512,4096]{1,0:T(8,128)(2,1)}, u32[]{:S(2)}, u32[]{:S(2)}) %collective-permute-start.1) | collective-permute-done | bytes 4194336 | tf_op jit(solution)/shard_map/ppermute | solution.py:725
  165.8 7.3 %add_convert_fusion.refs_19_ = bf16[512,4096]{1,0:T(8,128)(2,1)} fusion(bf16[512,4096]{1,0:T(8,128)(2,1)} %collective-permute-done.1, bf16[512,4096]{1,0:T(8,128)(2,1)} %get-tuple-element.113), kind=kLoop, calls=%fused_computation | loop fusion | flops 8388608 | bytes 12582912 | tf_op jit(solution)/shard_map/convert_element_type | solution.py:729
  173.0 12.0 %last.1 = (f32[512,512]{1,0:T(8,128)}, bf16[512,1152]{1,0:T(8,128)(2,1)}, bf16[512,1152]{1,0:T(8,128)(2,1)}) custom-call(s32[8]{0:T(128)} %pad_add_fusion.refs_0_, bf16[1024,7168]{1,0:T(8,128)(2,1)} %all-gather.3.cloned.1.call-done.refs_1_, f32[32,512]{1,0:T(8,128)} %get-tuple-element.68.refs_2_, f32[8,512]{1,0:T(8,128)} %get-tuple-element.97.refs_3_, ...), custom_call_target="tpu_custom_call" | custom-call | flops 10000000000 | bytes 10000000 | tf_op jit(solution)/shard_map/last/pallas_call | solution.py:628
  185.4 2.8 %collective-permute-done.2 = bf16[512,1152]{1,0:T(8,128)(2,1)S(1)} collective-permute-done((bf16[512,1152]{1,0:T(8,128)(2,1)}, bf16[512,1152]{1,0:T(8,128)(2,1)S(1)}, u32[]{:S(2)}, u32[]{:S(2)}) %collective-permute-start.2) | collective-permute-done | bytes 1179680 | tf_op jit(solution)/shard_map/ppermute | solution.py:725
  188.2 1.6 add_convert_fusion.2
  189.8 23.3 %all_to_all.15 = bf16[16,32,1152]{2,1,0:T(8,128)(2,1)S(1)} all-to-all(bf16[16,32,1152]{2,1,0:T(8,128)(2,1)S(1)} %bitcast.102), channel_id=1, replica_groups=mesh['x'=4,'y'=4,'z'=4,'c'=2] {'y','z'}, dimensions={0} | all-to-all | bytes 2359296 | tf_op jit(solution)/shard_map/all_to_all | solution.py:738
  213.3 3.6 %all-to-all-start.1 = ((bf16[16,8,2048]{2,1,0:T(8,128)(2,1)}), bf16[16,8,2048]{2,1,0:T(8,128)(2,1)S(1)}, u32[]{:S(2)}, u32[]{:S(2)}) async-start(bf16[16,8,2048]{2,1,0:T(8,128)(2,1)} %bitcast.29), calls=%async_computation.3 | async-start | bytes 1048576 | tf_op jit(solution)/shard_map/all_to_all | solution.py:738
  217.0 8.9 %all-to-all-done.1 = bf16[16,8,2048]{2,1,0:T(8,128)(2,1)S(1)} async-done(((bf16[16,8,2048]{2,1,0:T(8,128)(2,1)}), bf16[16,8,2048]{2,1,0:T(8,128)(2,1)S(1)}, u32[]{:S(2)}, u32[]{:S(2)}) %all-to-all-start.1) | async-done | bytes 524320 | tf_op jit(solution)/shard_map/all_to_all | solution.py:738
  225.9 4.3 %all-to-all-start.2 = ((bf16[16,8,4096]{2,1,0:T(8,128)(2,1)}), bf16[16,8,4096]{2,1,0:T(8,128)(2,1)S(1)}, u32[]{:S(2)}, u32[]{:S(2)}) async-start(bf16[16,8,4096]{2,1,0:T(8,128)(2,1)} %bitcast.103), calls=%async_computation.4 | async-start | bytes 2097152 | tf_op jit(solution)/shard_map/all_to_all | solution.py:738
  230.5 2.4 collective-permute-start.4
  232.9 1.1 collective-permute-start.5
  234.6 0.9 collective-permute-done.5
  236.0 0.7 copy.118
  238.0 6.4 %all-to-all-done.2 = bf16[16,8,4096]{2,1,0:T(8,128)(2,1)S(1)} async-done(((bf16[16,8,4096]{2,1,0:T(8,128)(2,1)}), bf16[16,8,4096]{2,1,0:T(8,128)(2,1)S(1)}, u32[]{:S(2)}, u32[]{:S(2)}) %all-to-all-start.2) | async-done | bytes 1048608 | tf_op jit(solution)/shard_map/all_to_all | solution.py:738
  245.5 3.9 %collective-permute-start.6 = (f32[4,10,512]{2,0,1:T(4,128)S(1)}, f32[4,10,512]{2,0,1:T(4,128)S(1)}, u32[]{:S(2)}, u32[]{:S(2)}) collective-permute-start(f32[4,10,512]{2,0,1:T(4,128)S(1)} %bitcast.115), channel_id=1, source_target_pairs={{0,1},{1,0},{2,3},{3,2},{4,5},{5,4},{6,7},{7,6},{8,9},{9,8},{10,11... | collective-permute-start | bytes 245768 | tf_op jit(solution)/shard_map/ppermute | solution.py:725
  250.6 0.7 reshape.157
  (72 shorter events, 10.3 us)
Async XLA Ops:
  7.2 43.6 %copy-start.1 = (s32[2,1]{0,1:T(1,128)S(1)}, s32[2,1]{0,1:T(1,128)}, u32[]{:S(2)}) copy-start(s32[2,1]{0,1:T(1,128)} %param.16) | copy-start | bytes 28
  7.2 43.6 %copy-start = (s32[2,1]{0,1:T(1,128)S(1)}, s32[2,1]{0,1:T(1,128)}, u32[]{:S(2)}) copy-start(s32[2,1]{0,1:T(1,128)} %param.17) | copy-start | bytes 28
  7.2 86.1 %all-gather.3.cloned.1.call-start = ((), (), s32[]{:S(2)}) async-start(), calls=%async_computation.5 | async-start | bytes 14794752 | tf_op jit(solution)/shard_map/all_gather | solution.py:756
  13.5 148.5 %reduce-scatter.3.cloned.1.call-start = ((), (), s32[]{:S(2)}) async-start(), calls=%async_computation.6 | async-start | bytes 2621440 | tf_op jit(solution)/shard_map/reduce_scatter | solution.py:733
  125.0 4.5 %collective-permute-start = (bf16[512,2048]{1,0:T(8,128)(2,1)}, bf16[512,2048]{1,0:T(8,128)(2,1)S(1)}, u32[]{:S(2)}, u32[]{:S(2)}) collective-permute-start(bf16[512,2048]{1,0:T(8,128)(2,1)} %get-tuple-element.96), channel_id=1, source_target_pairs={{0,1},{1,0},{2,3},{3,2},{4,5},{5,4},{6,7},{7,6},{8,9},{9,8},{10,11... | collective-permute-start | bytes 6291464 | tf_op jit(solution)/shard_map/ppermute | solution.py:725
  133.2 92.8 %reduce-scatter.5.cloned.1.call-start = ((), (), s32[]{:S(2)}) async-start(), calls=%async_computation.7 | async-start | bytes 5242880 | tf_op jit(solution)/shard_map/reduce_scatter | solution.py:733
  158.2 7.6 %collective-permute-start.1 = (bf16[512,4096]{1,0:T(8,128)(2,1)}, bf16[512,4096]{1,0:T(8,128)(2,1)}, u32[]{:S(2)}, u32[]{:S(2)}) collective-permute-start(bf16[512,4096]{1,0:T(8,128)(2,1)} %get-tuple-element.114), channel_id=1, source_target_pairs={{0,1},{1,0},{2,3},{3,2},{4,5},{5,4},{6,7},{7,6},{8,9},{9,8},{10,11... | collective-permute-start | bytes 12582920 | tf_op jit(solution)/shard_map/ppermute | solution.py:725
  185.1 3.1 %collective-permute-start.2 = (bf16[512,1152]{1,0:T(8,128)(2,1)}, bf16[512,1152]{1,0:T(8,128)(2,1)S(1)}, u32[]{:S(2)}, u32[]{:S(2)}) collective-permute-start(bf16[512,1152]{1,0:T(8,128)(2,1)} %get-tuple-element.119), channel_id=1, source_target_pairs={{0,1},{1,0},{2,3},{3,2},{4,5},{5,4},{6,7},{7,6},{8,9},{9,8},{10,11... | collective-permute-start | bytes 3538952 | tf_op jit(solution)/shard_map/ppermute | solution.py:725
  213.3 12.6 %all-to-all-start.1 = ((bf16[16,8,2048]{2,1,0:T(8,128)(2,1)}), bf16[16,8,2048]{2,1,0:T(8,128)(2,1)S(1)}, u32[]{:S(2)}, u32[]{:S(2)}) async-start(bf16[16,8,2048]{2,1,0:T(8,128)(2,1)} %bitcast.29), calls=%async_computation.3 | async-start | bytes 1048576 | tf_op jit(solution)/shard_map/all_to_all | solution.py:738
  225.9 18.5 %all-to-all-start.2 = ((bf16[16,8,4096]{2,1,0:T(8,128)(2,1)}), bf16[16,8,4096]{2,1,0:T(8,128)(2,1)S(1)}, u32[]{:S(2)}, u32[]{:S(2)}) async-start(bf16[16,8,4096]{2,1,0:T(8,128)(2,1)} %bitcast.103), calls=%async_computation.4 | async-start | bytes 2097152 | tf_op jit(solution)/shard_map/all_to_all | solution.py:738
  230.2 3.9 %collective-permute-start.3 = (bf16[8,1152]{1,0:T(8,128)(2,1)S(1)}, bf16[8,1152]{1,0:T(8,128)(2,1)S(1)}, u32[]{:S(2)}, u32[]{:S(2)}) collective-permute-start(bf16[8,1152]{1,0:T(8,128)(2,1)S(1)} %get-tuple-element.188), channel_id=1, source_target_pairs={{0,32},{32,64},{64,96},{96,0},{1,33},{33,65},{65,97},{97,1},{2,34}... | collective-permute-start | bytes 55304 | tf_op jit(solution)/shard_map/ppermute | solution.py:748
  230.5 4.1 %collective-permute-start.4 = (bf16[8,1152]{1,0:T(8,128)(2,1)S(1)}, bf16[8,1152]{1,0:T(8,128)(2,1)S(1)}, u32[]{:S(2)}, u32[]{:S(2)}) collective-permute-start(bf16[8,1152]{1,0:T(8,128)(2,1)S(1)} %get-tuple-element.190), channel_id=1, source_target_pairs={{0,64},{32,96},{64,0},{96,32},{1,65},{33,97},{65,1},{97,33},{2,66}... | collective-permute-start | bytes 55304 | tf_op jit(solution)/shard_map/ppermute | solution.py:748
  232.9 2.6 %collective-permute-start.5 = (bf16[8,1152]{1,0:T(8,128)(2,1)S(1)}, bf16[8,1152]{1,0:T(8,128)(2,1)S(1)}, u32[]{:S(2)}, u32[]{:S(2)}) collective-permute-start(bf16[8,1152]{1,0:T(8,128)(2,1)S(1)} %get-tuple-element.189), channel_id=1, source_target_pairs={{0,96},{32,0},{64,32},{96,64},{1,97},{33,1},{65,33},{97,65},{2,98}... | collective-permute-start | bytes 55304 | tf_op jit(solution)/shard_map/ppermute | solution.py:748
  245.5 4.8 %collective-permute-start.6 = (f32[4,10,512]{2,0,1:T(4,128)S(1)}, f32[4,10,512]{2,0,1:T(4,128)S(1)}, u32[]{:S(2)}, u32[]{:S(2)}) collective-permute-start(f32[4,10,512]{2,0,1:T(4,128)S(1)} %bitcast.115), channel_id=1, source_target_pairs={{0,1},{1,0},{2,3},{3,2},{4,5},{5,4},{6,7},{7,6},{8,9},{9,8},{10,11... | collective-permute-start | bytes 245768 | tf_op jit(solution)/shard_map/ppermute | solution.py:725
Sparse Core Ops, SparseCore 0:
  13.6 79.6 all-gather.2
  133.3 28.7 reduce-scatter.2
  173.2 45.8 reduce-scatter.4
